TPU v7x, 256 devices: a whole 4x4x8 slice. The times are simulated.
256 devices in a mesh: gx: 32 (over x, y, core), gz: 8 (over z).
Axes of the slice: x: 4, y: 4, z: 8, core: 2. Of those that a mesh axis runs over, the one named last changes fastest.
Arguments:
- potential: float32 [1024, 512, 128], P('gz', 'gx'), may hold values from -3 to 3
- negative_charges: float32 [1024, 512, 128], P('gz', 'gx'), may hold values from 0.1 to 10
- positive_charges: float32 [1024, 512, 128], P('gz', 'gx'), may hold values from 0.1 to 10
- vacancies: float32 [1024, 512, 128], P('gz', 'gx'), may hold values from 0.2 to 5
- permittivity: float32 [1024, 512, 128], P('gz', 'gx'), may hold values from 2 to 30
- doping: float32 [1024, 512, 128], P('gz', 'gx'), may hold values from -6 to 6
- optical_creation: float32 [1024, 512, 128], P('gz', 'gx'), may hold values from 0.1 to 4
- layer: int32 [1024], replicated, may hold values from 0 to 2, as said below
- height: int32 [512, 128], P('gx'), may hold values from 0 to 15
Outputs:
- potential_out: float32 [1024, 512, 128], P('gz', 'gx')
- electrons_out: float32 [1024, 512, 128], P('gz', 'gx')
- holes_out: float32 [1024, 512, 128], P('gz', 'gx')
- vacancies_out: float32 [1024, 512, 128], P('gz', 'gx')
Inputs may be any that keep to these rules, and one draw needn't show every extreme that they name: layer never falls along depth: 0 on the first levels, then 1 on a band of a few levels, then 2; all three values occur, and the first 1 lies at depth index under 3 * 128.
All inputs are finite; a program needn't handle non-finite values.
Results may differ from a plain program's by a relative error of at most 0.0003.
Values sent between devices are 32-bit elements; how exact they have to be, the bound alone decides.
A program may use at most 128 MiB of HBM per device.

v0:
```python
import jax
import jax.numpy as jnp
from jax import lax
from jax.sharding import PartitionSpec as P

ITERS = 4


POISSON_SCALE = 2.0
TIME_STEP = 0.05
DIFF_ELEC = 0.8
DIFF_HOLE = 0.6
DIFF_ION = 0.4


def extended_2(block, sides, width):
    for axis, dim in sides:
        count = lax.axis_size(axis)
        forward = [(i, i + 1) for i in range(count - 1)]
        backward = [(target, source) for source, target in forward]
        low = lax.ppermute(
            lax.slice_in_dim(block, block.shape[dim] - width, None, axis=dim), axis, forward
        )
        high = lax.ppermute(lax.slice_in_dim(block, 0, width, axis=dim), axis, backward)
        block = jnp.concatenate([low, block, high], axis=dim)
    return block


def bernoulli(value):
    small = jnp.abs(value) < 0.001
    safe = jnp.where(small, jnp.ones_like(value), jnp.expm1(value))
    return jnp.where(small, 1.0 - 0.5 * value + value * value / 12.0, value / safe)


def neighbours(extended):
    centre = extended[1:-1, 1:-1]
    return [
        extended[:-2, 1:-1],
        extended[2:, 1:-1],
        extended[1:-1, :-2],
        extended[1:-1, 2:],
        jnp.roll(centre, 1, axis=2),
        jnp.roll(centre, -1, axis=2),
    ]


def sweep(voltage_bordered, eps_ext, charge, outside):
    eps_centre = eps_ext[1:-1, 1:-1]
    numer = POISSON_SCALE * charge
    denom = outside
    for eps_next, psi_next in zip(neighbours(eps_ext), neighbours(voltage_bordered)):
        coef = 0.5 * (eps_centre + eps_next)
        numer = numer + coef * psi_next
        denom = denom + coef
    return numer / denom * (1.0 - outside)


def charged_populations(
    voltage_bordered, negative_bordered, positive_bordered, optical_creation, recombination_time
):
    psi_c = voltage_bordered[1:-1, 1:-1]
    negative_middle = negative_bordered[1:-1, 1:-1]
    positive_middle = positive_bordered[1:-1, 1:-1]
    out_elec = jnp.zeros_like(psi_c)
    out_hole = jnp.zeros_like(psi_c)
    floor_limits = []
    voltage_iterates = []
    for psi_n, elec_n, hole_n in zip(
        neighbours(voltage_bordered), neighbours(negative_bordered), neighbours(positive_bordered)
    ):
        delta = psi_n - psi_c
        lower = bernoulli(delta)
        upper = lower + delta
        out_elec = out_elec + (upper * negative_middle - lower * elec_n)
        out_hole = out_hole + (lower * positive_middle - upper * hole_n)
        floor_limits.append(lower)
        voltage_iterates.append(delta)
    annihilation_loss = (negative_middle * positive_middle - 1.0) / (
        recombination_time * (negative_middle + positive_middle + 2.0)
    )
    negative_population = (
        negative_middle
        - TIME_STEP * DIFF_ELEC * out_elec
        + TIME_STEP * (optical_creation - annihilation_loss)
    )
    positive_population = (
        positive_middle
        - TIME_STEP * DIFF_HOLE * out_hole
        + TIME_STEP * (optical_creation - annihilation_loss)
    )
    return (negative_population, positive_population, floor_limits, voltage_iterates)


def ion_update(ion_ext, pero_ext, floor_limits, voltage_iterates):
    ion_c = ion_ext[1:-1, 1:-1]
    pero_c = pero_ext[1:-1, 1:-1]
    out_ion = jnp.zeros_like(ion_c)
    for lower, delta, ion_n, pero_n in zip(
        floor_limits, voltage_iterates, neighbours(ion_ext), neighbours(pero_ext)
    ):
        upper = lower + delta
        out_ion = out_ion + (lower * ion_c - upper * ion_n) * (pero_c * pero_n)
    return ion_c - TIME_STEP * DIFF_ION * out_ion


def on_device(
    potential,
    negative_charges,
    positive_charges,
    vacancies,
    permittivity,
    doping,
    optical_creation,
    layer,
    height,
):
    depth_cells, width_cells, rows = potential.shape
    total_depth = depth_cells * lax.axis_size("gz")
    total_width = width_cells * lax.axis_size("gx")
    boundary = jnp.sum((layer == 0).astype(jnp.int32))
    junction_end = jnp.sum((layer <= 1).astype(jnp.int32))
    depth_first = lax.axis_index("gz") * depth_cells
    width_first = lax.axis_index("gx") * width_cells
    height_ext = extended_2(height, (("gx", 0),), 1)
    zpos = depth_first - 1 + jnp.arange(depth_cells + 2, dtype=jnp.int32)
    xpos = width_first - 1 + jnp.arange(width_cells + 2, dtype=jnp.int32)
    inside = ((zpos >= 0) & (zpos < total_depth))[:, None, None] & (
        (xpos >= 0) & (xpos < total_width)
    )[None, :, None]
    level = zpos[:, None, None] + height_ext[None]
    pero_ext = ((level < boundary) & inside).astype(jnp.float32)
    level_centre = level[1:-1, 1:-1]
    absorber_middle = pero_ext[1:-1, 1:-1]
    interface_plane = (level_centre >= boundary) & (level_centre < junction_end)
    recombination_time = jnp.where(
        absorber_middle > 0.0, 1.0, jnp.where(interface_plane, 0.1, 5.0)
    ).astype(jnp.float32)
    ions = vacancies * absorber_middle
    charge = positive_charges - negative_charges + ions + doping
    psi = potential
    negative_bordered, positive_bordered, ion_ext, eps_ext = (
        extended_2(negative_charges, (("gx", 1), ("gz", 0)), 1),
        extended_2(positive_charges, (("gx", 1), ("gz", 0)), 1),
        extended_2(ions, (("gx", 1), ("gz", 0)), 1),
        extended_2(permittivity, (("gx", 1), ("gz", 0)), 1),
    )
    for sweep_index in range(ITERS):
        voltage_bordered = extended_2(psi, (("gx", 1), ("gz", 0)), 1)
        psi = sweep(voltage_bordered, eps_ext, charge, 0.0)
    voltage_solution = extended_2(psi, (("gx", 1), ("gz", 0)), 1)
    negative_population, positive_population, floor_limits, voltage_iterates = charged_populations(
        voltage_solution, negative_bordered, positive_bordered, optical_creation, recombination_time
    )
    ion = ion_update(ion_ext, pero_ext, floor_limits, voltage_iterates)
    return (psi, negative_population, positive_population, ion)


def solution(mesh):
    in_specs = (
        P("gz", "gx", None),
        P("gz", "gx", None),
        P("gz", "gx", None),
        P("gz", "gx", None),
        P("gz", "gx", None),
        P("gz", "gx", None),
        P("gz", "gx", None),
        P(),
        P("gx", None),
    )
    out_specs = (P("gz", "gx", None), P("gz", "gx", None), P("gz", "gx", None), P("gz", "gx", None))
    return jax.shard_map(
        on_device, mesh=mesh, in_specs=in_specs, out_specs=out_specs, check_vma=False
    )
```

profile of v0, /device:TPU:6, one launch (start us, length us, event | category | flops | bytes accessed | tf_op | source)
XLA Modules:
  0.0 222.1 jit_solution(16418295807916224212)
XLA Ops:
  3.8 5.8 %collective-permute-start.1 = (s32[1,128]{1,0:T(1,128)}, s32[1,128]{1,0:T(1,128)}, u32[]{:S(2)}, u32[]{:S(2)}) collective-permute-start(s32[1,128]{1,0:T(1,128)} %get-tuple-element.88), channel_id=1, source_target_pairs={{8,0},{16,8},{24,16},{32,24},{40,32},{48,40},{56,48},{64,56},{72,6... | collective-permute-start | bytes 1544 | tf_op jit(solution)/shard_map/ppermute | solution.py:24
  13.5 5.8 %collective-permute-start.3 = (f32[128,1,128]{2,1,0:T(1,128)}, f32[128,1,128]{2,1,0:T(1,128)S(1)}, u32[]{:S(2)}, u32[]{:S(2)}) collective-permute-start(f32[128,1,128]{2,1,0:T(1,128)} %get-tuple-element.79), channel_id=1, source_target_pairs={{8,0},{16,8},{24,16},{32,24},{40,32},{48,40},{56,48},{64,56},{72,6... | collective-permute-start | bytes 196616 | tf_op jit(solution)/shard_map/ppermute | solution.py:24
  23.1 5.1 %fusion.144 = (f32[128,16,1]{2,1,0:T(8,128)}, f32[128,16,1]{2,1,0:T(8,128)}, f32[128,16,1]{2,1,0:T(8,128)}, f32[128,16,1]{2,1,0:T(8,128)}) fusion(f32[128,16,128]{2,1,0:T(8,128)} %param.13, f32[128,16,128]{2,1,0:T(8,128)} %param.9), kind=kLoop, calls=%fused_computation.292 | loop fusion | bytes 65536 | tf_op jit(solution)/shard_map/jit(_roll_static)/slice | solution.py:42
  40.4 5.8 %collective-permute-start.6 = (f32[128,1,128]{2,1,0:T(1,128)}, f32[128,1,128]{2,1,0:T(1,128)S(1)}, u32[]{:S(2)}, u32[]{:S(2)}) collective-permute-start(f32[128,1,128]{2,1,0:T(1,128)} %get-tuple-element.86), channel_id=1, source_target_pairs={{8,0},{16,8},{24,16},{32,24},{40,32},{48,40},{56,48},{64,56},{72,6... | collective-permute-start | bytes 196616 | tf_op jit(solution)/shard_map/ppermute | solution.py:24
  51.1 6.0 %collective-permute-start.31 = (f32[128,1,128]{2,1,0:T(1,128)S(1)}, f32[128,1,128]{2,1,0:T(1,128)S(1)}, u32[]{:S(2)}, u32[]{:S(2)}) collective-permute-start(f32[128,1,128]{2,1,0:T(1,128)S(1)} %get-tuple-element.56), channel_id=1, source_target_pairs={{8,0},{16,8},{24,16},{32,24},{40,32},{48,40},{56,48},{64,56},{72,6... | collective-permute-start | bytes 196616 | tf_op jit(solution)/shard_map/ppermute | solution.py:24
  59.1 5.9 %collective-permute-start.26 = (f32[128,1,128]{2,1,0:T(1,128)S(1)}, f32[128,1,128]{2,1,0:T(1,128)S(1)}, u32[]{:S(2)}, u32[]{:S(2)}) collective-permute-start(f32[128,1,128]{2,1,0:T(1,128)S(1)} %get-tuple-element.44), channel_id=1, source_target_pairs={{8,0},{16,8},{24,16},{32,24},{40,32},{48,40},{56,48},{64,56},{72,6... | collective-permute-start | bytes 196616 | tf_op jit(solution)/shard_map/ppermute | solution.py:24
  65.0 4.1 %collective-permute-start.4 = (f32[1,18,128]{2,1,0:T(8,128)S(1)}, f32[1,18,128]{2,1,0:T(8,128)S(1)}, u32[]{:S(2)}, u32[]{:S(2)}) collective-permute-start(f32[1,18,128]{2,1,0:T(8,128)S(1)} %get-tuple-element.30), channel_id=1, source_target_pairs={{0,1},{1,2},{2,3},{3,4},{4,5},{5,6},{6,7},{8,9},{9,10},{10,11},{11... | collective-permute-start | bytes 27656 | tf_op jit(solution)/shard_map/ppermute | solution.py:21
  70.5 4.5 %collective-permute-start.7 = (f32[1,18,128]{2,1,0:T(8,128)S(1)}, f32[1,18,128]{2,1,0:T(8,128)S(1)}, u32[]{:S(2)}, u32[]{:S(2)}) collective-permute-start(f32[1,18,128]{2,1,0:T(8,128)S(1)} %get-tuple-element.31), channel_id=1, source_target_pairs={{0,1},{1,2},{2,3},{3,4},{4,5},{5,6},{6,7},{8,9},{9,10},{10,11},{11... | collective-permute-start | bytes 27656 | tf_op jit(solution)/shard_map/ppermute | solution.py:21
  76.4 4.5 %collective-permute-start.32 = (f32[1,18,128]{2,1,0:T(8,128)S(1)}, f32[1,18,128]{2,1,0:T(8,128)S(1)}, u32[]{:S(2)}, u32[]{:S(2)}) collective-permute-start(f32[1,18,128]{2,1,0:T(8,128)S(1)} %get-tuple-element.21), channel_id=1, source_target_pairs={{0,1},{1,2},{2,3},{3,4},{4,5},{5,6},{6,7},{8,9},{9,10},{10,11},{11... | collective-permute-start | bytes 27656 | tf_op jit(solution)/shard_map/ppermute | solution.py:21
  82.3 5.5 %collective-permute-start.27 = (f32[1,18,128]{2,1,0:T(8,128)S(1)}, f32[1,18,128]{2,1,0:T(8,128)S(1)}, u32[]{:S(2)}, u32[]{:S(2)}) collective-permute-start(f32[1,18,128]{2,1,0:T(8,128)S(1)} %get-tuple-element.17), channel_id=1, source_target_pairs={{0,1},{1,2},{2,3},{3,4},{4,5},{5,6},{6,7},{8,9},{9,10},{10,11},{11... | collective-permute-start | bytes 27656 | tf_op jit(solution)/shard_map/ppermute | solution.py:21
  95.0 5.8 %collective-permute-start.11 = (f32[128,1,128]{2,1,0:T(1,128)S(1)}, f32[128,1,128]{2,1,0:T(1,128)S(1)}, u32[]{:S(2)}, u32[]{:S(2)}) collective-permute-start(f32[128,1,128]{2,1,0:T(1,128)S(1)} %get-tuple-element.74), channel_id=1, source_target_pairs={{8,0},{16,8},{24,16},{32,24},{40,32},{48,40},{56,48},{64,56},{72,6... | collective-permute-start | bytes 196616 | tf_op jit(solution)/shard_map/ppermute | solution.py:24
  102.8 5.8 %collective-permute-start.35 = (f32[128,1,128]{2,1,0:T(1,128)S(1)}, f32[128,1,128]{2,1,0:T(1,128)S(1)}, u32[]{:S(2)}, u32[]{:S(2)}) collective-permute-start(f32[128,1,128]{2,1,0:T(1,128)S(1)} %get-tuple-element.38), channel_id=1, source_target_pairs={{8,0},{16,8},{24,16},{32,24},{40,32},{48,40},{56,48},{64,56},{72,6... | collective-permute-start | bytes 196616 | tf_op jit(solution)/shard_map/ppermute | solution.py:24
  108.6 5.1 %collective-permute-start.12 = (f32[1,18,128]{2,1,0:T(8,128)S(1)}, f32[1,18,128]{2,1,0:T(8,128)S(1)}, u32[]{:S(2)}, u32[]{:S(2)}) collective-permute-start(f32[1,18,128]{2,1,0:T(8,128)S(1)} %get-tuple-element.27), channel_id=1, source_target_pairs={{0,1},{1,2},{2,3},{3,4},{4,5},{5,6},{6,7},{8,9},{9,10},{10,11},{11... | collective-permute-start | bytes 27656 | tf_op jit(solution)/shard_map/ppermute | solution.py:21
  115.2 5.4 %collective-permute-done.13 = f32[1,18,128]{2,1,0:T(8,128)S(1)} collective-permute-done((f32[1,18,128]{2,1,0:T(8,128)S(1)}, f32[1,18,128]{2,1,0:T(8,128)S(1)}, u32[]{:S(2)}, u32[]{:S(2)}) %collective-permute-start.13) | collective-permute-done | bytes 9248 | tf_op jit(solution)/shard_map/ppermute | solution.py:24
  126.0 5.8 %collective-permute-start.15 = (f32[128,1,128]{2,1,0:T(1,128)S(1)}, f32[128,1,128]{2,1,0:T(1,128)S(1)}, u32[]{:S(2)}, u32[]{:S(2)}) collective-permute-start(f32[128,1,128]{2,1,0:T(1,128)S(1)} %get-tuple-element.68), channel_id=1, source_target_pairs={{8,0},{16,8},{24,16},{32,24},{40,32},{48,40},{56,48},{64,56},{72,6... | collective-permute-start | bytes 196616 | tf_op jit(solution)/shard_map/ppermute | solution.py:24
  133.6 5.1 %collective-permute-start.16 = (f32[1,18,128]{2,1,0:T(8,128)S(1)}, f32[1,18,128]{2,1,0:T(8,128)S(1)}, u32[]{:S(2)}, u32[]{:S(2)}) collective-permute-start(f32[1,18,128]{2,1,0:T(8,128)S(1)} %get-tuple-element.25), channel_id=1, source_target_pairs={{0,1},{1,2},{2,3},{3,4},{4,5},{5,6},{6,7},{8,9},{9,10},{10,11},{11... | collective-permute-start | bytes 27656 | tf_op jit(solution)/shard_map/ppermute | solution.py:21
  149.7 5.8 %collective-permute-start.19 = (f32[128,1,128]{2,1,0:T(1,128)S(1)}, f32[128,1,128]{2,1,0:T(1,128)S(1)}, u32[]{:S(2)}, u32[]{:S(2)}) collective-permute-start(f32[128,1,128]{2,1,0:T(1,128)S(1)} %get-tuple-element.62), channel_id=1, source_target_pairs={{8,0},{16,8},{24,16},{32,24},{40,32},{48,40},{56,48},{64,56},{72,6... | collective-permute-start | bytes 196616 | tf_op jit(solution)/shard_map/ppermute | solution.py:24
  157.4 3.9 %collective-permute-start.20 = (f32[1,18,128]{2,1,0:T(8,128)S(1)}, f32[1,18,128]{2,1,0:T(8,128)S(1)}, u32[]{:S(2)}, u32[]{:S(2)}) collective-permute-start(f32[1,18,128]{2,1,0:T(8,128)S(1)} %get-tuple-element.23), channel_id=1, source_target_pairs={{0,1},{1,2},{2,3},{3,4},{4,5},{5,6},{6,7},{8,9},{9,10},{10,11},{11... | collective-permute-start | bytes 27656 | tf_op jit(solution)/shard_map/ppermute | solution.py:21
  162.9 3.9 %collective-permute-done.21 = f32[1,18,128]{2,1,0:T(8,128)S(1)} collective-permute-done((f32[1,18,128]{2,1,0:T(8,128)S(1)}, f32[1,18,128]{2,1,0:T(8,128)S(1)}, u32[]{:S(2)}, u32[]{:S(2)}) %collective-permute-start.21) | collective-permute-done | bytes 9248 | tf_op jit(solution)/shard_map/ppermute | solution.py:24
  172.2 5.8 %collective-permute-start.23 = (f32[128,1,128]{2,1,0:T(1,128)S(1)}, f32[128,1,128]{2,1,0:T(1,128)S(1)}, u32[]{:S(2)}, u32[]{:S(2)}) collective-permute-start(f32[128,1,128]{2,1,0:T(1,128)S(1)} %get-tuple-element.49), channel_id=1, source_target_pairs={{8,0},{16,8},{24,16},{32,24},{40,32},{48,40},{56,48},{64,56},{72,6... | collective-permute-start | bytes 196616 | tf_op jit(solution)/shard_map/ppermute | solution.py:24
  186.3 5.2 %collective-permute-start.36 = (f32[1,18,128]{2,1,0:T(8,128)S(1)}, f32[1,18,128]{2,1,0:T(8,128)S(1)}, u32[]{:S(2)}, u32[]{:S(2)}) collective-permute-start(f32[1,18,128]{2,1,0:T(8,128)S(1)} %get-tuple-element.15), channel_id=1, source_target_pairs={{0,1},{1,2},{2,3},{3,4},{4,5},{5,6},{6,7},{8,9},{9,10},{10,11},{11... | collective-permute-start | bytes 27656 | tf_op jit(solution)/shard_map/ppermute | solution.py:21
  192.9 11.0 %fusion.26 = (f32[128,16,128]{2,1,0:T(8,128)}, f32[128,16,128]{2,1,0:T(8,128)S(1)}) fusion(f32[128,16,128]{2,1,0:T(8,128)S(1)} %copy-done.3, f32[128,1,128]{2,1,0:T(1,128)S(1)} %collective-permute-done.31, f32[128,1,128]{2,1,0:T(1,128)S(1)} %collective-permute-done.30, f32[1,18,128]{2,1,0:T(8,128)S(1)} %collective-permute-done.33, ...), kind=kLoop, calls=%fused_computation.40 | loop fusion | flops 34603008 | bytes 12881928 | tf_op jit(solution)/shard_map/add | solution.py:87
  204.0 8.5 %fusion.42 = f32[128,16,128]{2,1,0:T(8,128)} fusion(f32[128,16,128]{2,1,0:T(8,128)S(1)} %get-tuple-element.7, f32[128,16,128]{2,1,0:T(8,128)S(1)} %copy-done.2, f32[128,1,128]{2,1,0:T(1,128)S(1)} %collective-permute-done.26, f32[128,1,128]{2,1,0:T(1,128)S(1)} %collective-permute-done.25, f32[1,18,128]{2,1,0:T(8,128)S(1)} %collective-permute-done.29, ...), kind=kLoop, calls=%fused_computation.64 | loop fusion | flops 30932992 | bytes 8687616 | tf_op jit(solution)/shard_map/add | solution.py:82
  212.5 9.6 %fusion.5 = f32[128,16,128]{2,1,0:T(8,128)} fusion(f32[128,16,128]{2,1,0:T(8,128)S(1)} %get-tuple-element.10, f32[130,18,128]{2,1,0:T(8,128)S(1)} %and_convert_fusion, f32[128,1,128]{2,1,0:T(1,128)S(1)} %collective-permute-done.35, f32[128,1,128]{2,1,0:T(1,128)S(1)} %collective-permute-done.34, f32[1,18,128]{2,1,0:T(8,128)S(1)} %collective-permute-done.37, ...), kind=kLoop, calls=%fused_computation.7 | loop fusion | flops 34340864 | bytes 14979072 | tf_op jit(solution)/shard_map/sub | solution.py:103
  (158 shorter events, 80.9 us)
Async XLA Ops:
  1.9 38.5 %collective-permute-start = (s32[1,128]{1,0:T(1,128)}, s32[1,128]{1,0:T(1,128)S(1)}, u32[]{:S(2)}, u32[]{:S(2)}) collective-permute-start(s32[1,128]{1,0:T(1,128)} %get-tuple-element.87), channel_id=1, source_target_pairs={{0,8},{8,16},{16,24},{24,32},{32,40},{40,48},{48,56},{56,64},{64,7... | collective-permute-start | bytes 1544 | tf_op jit(solution)/shard_map/ppermute | solution.py:21
  3.8 42.4 %collective-permute-start.1 = (s32[1,128]{1,0:T(1,128)}, s32[1,128]{1,0:T(1,128)}, u32[]{:S(2)}, u32[]{:S(2)}) collective-permute-start(s32[1,128]{1,0:T(1,128)} %get-tuple-element.88), channel_id=1, source_target_pairs={{8,0},{16,8},{24,16},{32,24},{40,32},{48,40},{56,48},{64,56},{72,6... | collective-permute-start | bytes 1544 | tf_op jit(solution)/shard_map/ppermute | solution.py:24
  11.6 39.5 %collective-permute-start.2 = (f32[128,1,128]{2,1,0:T(1,128)}, f32[128,1,128]{2,1,0:T(1,128)S(1)}, u32[]{:S(2)}, u32[]{:S(2)}) collective-permute-start(f32[128,1,128]{2,1,0:T(1,128)} %get-tuple-element.80), channel_id=1, source_target_pairs={{0,8},{8,16},{16,24},{24,32},{32,40},{40,48},{48,56},{56,64},{64,7... | collective-permute-start | bytes 196616 | tf_op jit(solution)/shard_map/ppermute | solution.py:21
  13.5 43.6 %collective-permute-start.3 = (f32[128,1,128]{2,1,0:T(1,128)}, f32[128,1,128]{2,1,0:T(1,128)S(1)}, u32[]{:S(2)}, u32[]{:S(2)}) collective-permute-start(f32[128,1,128]{2,1,0:T(1,128)} %get-tuple-element.79), channel_id=1, source_target_pairs={{8,0},{16,8},{24,16},{32,24},{40,32},{48,40},{56,48},{64,56},{72,6... | collective-permute-start | bytes 196616 | tf_op jit(solution)/shard_map/ppermute | solution.py:24
  21.2 37.9 %collective-permute-start.5 = (f32[128,1,128]{2,1,0:T(1,128)}, f32[128,1,128]{2,1,0:T(1,128)S(1)}, u32[]{:S(2)}, u32[]{:S(2)}) collective-permute-start(f32[128,1,128]{2,1,0:T(1,128)} %get-tuple-element.85), channel_id=1, source_target_pairs={{0,8},{8,16},{16,24},{24,32},{32,40},{40,48},{48,56},{56,64},{64,7... | collective-permute-start | bytes 196616 | tf_op jit(solution)/shard_map/ppermute | solution.py:21
  40.4 24.5 %collective-permute-start.6 = (f32[128,1,128]{2,1,0:T(1,128)}, f32[128,1,128]{2,1,0:T(1,128)S(1)}, u32[]{:S(2)}, u32[]{:S(2)}) collective-permute-start(f32[128,1,128]{2,1,0:T(1,128)} %get-tuple-element.86), channel_id=1, source_target_pairs={{8,0},{16,8},{24,16},{32,24},{40,32},{48,40},{56,48},{64,56},{72,6... | collective-permute-start | bytes 196616 | tf_op jit(solution)/shard_map/ppermute | solution.py:24
  46.2 22.9 %collective-permute-start.30 = (f32[128,1,128]{2,1,0:T(1,128)}, f32[128,1,128]{2,1,0:T(1,128)S(1)}, u32[]{:S(2)}, u32[]{:S(2)}) collective-permute-start(f32[128,1,128]{2,1,0:T(1,128)} %get-tuple-element.55), channel_id=1, source_target_pairs={{0,8},{8,16},{16,24},{24,32},{32,40},{40,48},{48,56},{56,64},{64,7... | collective-permute-start | bytes 196616 | tf_op jit(solution)/shard_map/ppermute | solution.py:21
  51.1 19.4 %collective-permute-start.31 = (f32[128,1,128]{2,1,0:T(1,128)S(1)}, f32[128,1,128]{2,1,0:T(1,128)S(1)}, u32[]{:S(2)}, u32[]{:S(2)}) collective-permute-start(f32[128,1,128]{2,1,0:T(1,128)S(1)} %get-tuple-element.56), channel_id=1, source_target_pairs={{8,0},{16,8},{24,16},{32,24},{40,32},{48,40},{56,48},{64,56},{72,6... | collective-permute-start | bytes 196616 | tf_op jit(solution)/shard_map/ppermute | solution.py:24
  57.1 17.9 %collective-permute-start.25 = (f32[128,1,128]{2,1,0:T(1,128)S(1)}, f32[128,1,128]{2,1,0:T(1,128)S(1)}, u32[]{:S(2)}, u32[]{:S(2)}) collective-permute-start(f32[128,1,128]{2,1,0:T(1,128)S(1)} %get-tuple-element.43), channel_id=1, source_target_pairs={{0,8},{8,16},{16,24},{24,32},{32,40},{40,48},{48,56},{56,64},{64,7... | collective-permute-start | bytes 196616 | tf_op jit(solution)/shard_map/ppermute | solution.py:21
  59.1 17.3 %collective-permute-start.26 = (f32[128,1,128]{2,1,0:T(1,128)S(1)}, f32[128,1,128]{2,1,0:T(1,128)S(1)}, u32[]{:S(2)}, u32[]{:S(2)}) collective-permute-start(f32[128,1,128]{2,1,0:T(1,128)S(1)} %get-tuple-element.44), channel_id=1, source_target_pairs={{8,0},{16,8},{24,16},{32,24},{40,32},{48,40},{56,48},{64,56},{72,6... | collective-permute-start | bytes 196616 | tf_op jit(solution)/shard_map/ppermute | solution.py:24
  65.0 15.9 %collective-permute-start.4 = (f32[1,18,128]{2,1,0:T(8,128)S(1)}, f32[1,18,128]{2,1,0:T(8,128)S(1)}, u32[]{:S(2)}, u32[]{:S(2)}) collective-permute-start(f32[1,18,128]{2,1,0:T(8,128)S(1)} %get-tuple-element.30), channel_id=1, source_target_pairs={{0,1},{1,2},{2,3},{3,4},{4,5},{5,6},{6,7},{8,9},{9,10},{10,11},{11... | collective-permute-start | bytes 27656 | tf_op jit(solution)/shard_map/ppermute | solution.py:21
  69.2 13.1 %collective-permute-start.8 = (f32[1,18,128]{2,1,0:T(8,128)S(1)}, f32[1,18,128]{2,1,0:T(8,128)S(1)}, u32[]{:S(2)}, u32[]{:S(2)}) collective-permute-start(f32[1,18,128]{2,1,0:T(8,128)S(1)} %get-tuple-element.29), channel_id=1, source_target_pairs={{1,0},{2,1},{3,2},{4,3},{5,4},{6,5},{7,6},{9,8},{10,9},{11,10},{12... | collective-permute-start | bytes 27656 | tf_op jit(solution)/shard_map/ppermute | solution.py:24
  70.5 17.3 %collective-permute-start.7 = (f32[1,18,128]{2,1,0:T(8,128)S(1)}, f32[1,18,128]{2,1,0:T(8,128)S(1)}, u32[]{:S(2)}, u32[]{:S(2)}) collective-permute-start(f32[1,18,128]{2,1,0:T(8,128)S(1)} %get-tuple-element.31), channel_id=1, source_target_pairs={{0,1},{1,2},{2,3},{3,4},{4,5},{5,6},{6,7},{8,9},{9,10},{10,11},{11... | collective-permute-start | bytes 27656 | tf_op jit(solution)/shard_map/ppermute | solution.py:21
  75.0 12.7 %collective-permute-start.9 = (f32[1,18,128]{2,1,0:T(8,128)S(1)}, f32[1,18,128]{2,1,0:T(8,128)S(1)}, u32[]{:S(2)}, u32[]{:S(2)}) collective-permute-start(f32[1,18,128]{2,1,0:T(8,128)S(1)} %get-tuple-element.32), channel_id=1, source_target_pairs={{1,0},{2,1},{3,2},{4,3},{5,4},{6,5},{7,6},{9,8},{10,9},{11,10},{12... | collective-permute-start | bytes 27656 | tf_op jit(solution)/shard_map/ppermute | solution.py:24
  76.4 108.6 %collective-permute-start.32 = (f32[1,18,128]{2,1,0:T(8,128)S(1)}, f32[1,18,128]{2,1,0:T(8,128)S(1)}, u32[]{:S(2)}, u32[]{:S(2)}) collective-permute-start(f32[1,18,128]{2,1,0:T(8,128)S(1)} %get-tuple-element.21), channel_id=1, source_target_pairs={{0,1},{1,2},{2,3},{3,4},{4,5},{5,6},{6,7},{8,9},{9,10},{10,11},{11... | collective-permute-start | bytes 27656 | tf_op jit(solution)/shard_map/ppermute | solution.py:21
  80.9 105.3 %collective-permute-start.33 = (f32[1,18,128]{2,1,0:T(8,128)S(1)}, f32[1,18,128]{2,1,0:T(8,128)S(1)}, u32[]{:S(2)}, u32[]{:S(2)}) collective-permute-start(f32[1,18,128]{2,1,0:T(8,128)S(1)} %get-tuple-element.22), channel_id=1, source_target_pairs={{1,0},{2,1},{3,2},{4,3},{5,4},{6,5},{7,6},{9,8},{10,9},{11,10},{12... | collective-permute-start | bytes 27656 | tf_op jit(solution)/shard_map/ppermute | solution.py:24
  82.3 121.7 %collective-permute-start.27 = (f32[1,18,128]{2,1,0:T(8,128)S(1)}, f32[1,18,128]{2,1,0:T(8,128)S(1)}, u32[]{:S(2)}, u32[]{:S(2)}) collective-permute-start(f32[1,18,128]{2,1,0:T(8,128)S(1)} %get-tuple-element.17), channel_id=1, source_target_pairs={{0,1},{1,2},{2,3},{3,4},{4,5},{5,6},{6,7},{8,9},{9,10},{10,11},{11... | collective-permute-start | bytes 27656 | tf_op jit(solution)/shard_map/ppermute | solution.py:21
  102.8 10.9 %collective-permute-start.35 = (f32[128,1,128]{2,1,0:T(1,128)S(1)}, f32[128,1,128]{2,1,0:T(1,128)S(1)}, u32[]{:S(2)}, u32[]{:S(2)}) collective-permute-start(f32[128,1,128]{2,1,0:T(1,128)S(1)} %get-tuple-element.38), channel_id=1, source_target_pairs={{8,0},{16,8},{24,16},{32,24},{40,32},{48,40},{56,48},{64,56},{72,6... | collective-permute-start | bytes 196616 | tf_op jit(solution)/shard_map/ppermute | solution.py:24
  170.3 8.0 %collective-permute-start.22 = (f32[128,1,128]{2,1,0:T(1,128)S(1)}, f32[128,1,128]{2,1,0:T(1,128)S(1)}, u32[]{:S(2)}, u32[]{:S(2)}) collective-permute-start(f32[128,1,128]{2,1,0:T(1,128)S(1)} %get-tuple-element.50), channel_id=1, source_target_pairs={{0,8},{8,16},{16,24},{24,32},{32,40},{40,48},{48,56},{56,64},{64,7... | collective-permute-start | bytes 196616 | tf_op jit(solution)/shard_map/ppermute | solution.py:21
  179.9 11.6 %collective-permute-start.24 = (f32[1,18,128]{2,1,0:T(8,128)S(1)}, f32[1,18,128]{2,1,0:T(8,128)S(1)}, u32[]{:S(2)}, u32[]{:S(2)}) collective-permute-start(f32[1,18,128]{2,1,0:T(8,128)S(1)} %get-tuple-element.20), channel_id=1, source_target_pairs={{0,1},{1,2},{2,3},{3,4},{4,5},{5,6},{6,7},{8,9},{9,10},{10,11},{11... | collective-permute-start | bytes 27656 | tf_op jit(solution)/shard_map/ppermute | solution.py:21
  183.1 9.7 %collective-permute-start.28 = (f32[1,18,128]{2,1,0:T(8,128)S(1)}, f32[1,18,128]{2,1,0:T(8,128)S(1)}, u32[]{:S(2)}, u32[]{:S(2)}) collective-permute-start(f32[1,18,128]{2,1,0:T(8,128)S(1)} %get-tuple-element.19), channel_id=1, source_target_pairs={{1,0},{2,1},{3,2},{4,3},{5,4},{6,5},{7,6},{9,8},{10,9},{11,10},{12... | collective-permute-start | bytes 27656 | tf_op jit(solution)/shard_map/ppermute | solution.py:24
  185.0 18.9 %collective-permute-start.29 = (f32[1,18,128]{2,1,0:T(8,128)S(1)}, f32[1,18,128]{2,1,0:T(8,128)S(1)}, u32[]{:S(2)}, u32[]{:S(2)}) collective-permute-start(f32[1,18,128]{2,1,0:T(8,128)S(1)} %get-tuple-element.18), channel_id=1, source_target_pairs={{1,0},{2,1},{3,2},{4,3},{5,4},{6,5},{7,6},{9,8},{10,9},{11,10},{12... | collective-permute-start | bytes 27656 | tf_op jit(solution)/shard_map/ppermute | solution.py:24
  186.3 26.2 %collective-permute-start.36 = (f32[1,18,128]{2,1,0:T(8,128)S(1)}, f32[1,18,128]{2,1,0:T(8,128)S(1)}, u32[]{:S(2)}, u32[]{:S(2)}) collective-permute-start(f32[1,18,128]{2,1,0:T(8,128)S(1)} %get-tuple-element.15), channel_id=1, source_target_pairs={{0,1},{1,2},{2,3},{3,4},{4,5},{5,6},{6,7},{8,9},{9,10},{10,11},{11... | collective-permute-start | bytes 27656 | tf_op jit(solution)/shard_map/ppermute | solution.py:21
  191.5 21.0 %collective-permute-start.37 = (f32[1,18,128]{2,1,0:T(8,128)S(1)}, f32[1,18,128]{2,1,0:T(8,128)S(1)}, u32[]{:S(2)}, u32[]{:S(2)}) collective-permute-start(f32[1,18,128]{2,1,0:T(8,128)S(1)} %get-tuple-element.16), channel_id=1, source_target_pairs={{1,0},{2,1},{3,2},{4,3},{5,4},{6,5},{7,6},{9,8},{10,9},{11,10},{12... | collective-permute-start | bytes 27656 | tf_op jit(solution)/shard_map/ppermute | solution.py:24
  (41 other events, 607.8 us)
where the time goes:
time: 224 us; the launch traced here: 222 us
  starting transfers between devices  130 us (58%)
  other arithmetic  47.1 us (21%)
  local copies, waits for them, and re-layouts  25.2 us (11%)
  waiting for transfers between devices  17.9 us (8%)
    ppermute x19, starting transfers between devices, extended_2(): lax.ppermute(lax.slice_in_dim(block, 0, width, axis=dim), axis, backward)  70 us
    ppermute x19, starting transfers between devices, extended_2(): lax.ppermute(lax.slice_in_dim(block, block.shape[dim] - width, None, axis...  60.3 us
    ppermute x19, waiting for transfers between devices, extended_2(): lax.ppermute(lax.slice_in_dim(block, 0, width, axis=dim), axis, backward)  17.7 us
    div x4, other arithmetic, sweep(): return numer / denom * (1.0 - outside)  13.8 us
    add x1, other arithmetic, charged_populations(): positive_middle - TIME_STEP * DIFF_HOLE * out_hole  11 us
    slice x14, local copies, waits for them, and re-layouts, neighbours(): jnp.roll(centre, -1, axis=2)  10.2 us
    sub x1, other arithmetic, ion_update(): return ion_c - TIME_STEP * DIFF_ION * out_ion  9.61 us
    add x1, other arithmetic, charged_populations(): negative_middle - TIME_STEP * DIFF_ELEC * out_elec  8.54 us
  transfers between devices with their start and end apart: 38, of which 7 were waited for; matrix products, arithmetic and copies ran while one was open for 28% of the time, Pallas kernels for 0%

commit v1 on v0

v1 whole, which is shorter than its diff:
```python
import functools

import jax
import jax.numpy as jnp
from jax import lax
from jax.experimental import pallas as pl
from jax.experimental.pallas import tpu as pltpu
from jax.sharding import PartitionSpec as P

MESH = pl.DeviceIdType.MESH
F32 = jnp.float32

NXL = 16
NZL = 128
NY = 128
XO = 3
ZO = 16
PLANES = NXL + 2 * XO
ROWS = NZL + 2 * ZO
LO = ZO - 8
HI = ZO + NZL + 8
SPAN = HI - LO
TINY = 1e-10

XROWS = (ZO, ZO + NZL)
EROWS = (LO, HI)


def x_message(width, first, rows):
    low = XO - first - width
    return (
        ((XO + NXL - first - width, low, width), rows),
        ((XO + first, XO + NXL + first, width), rows),
    )


def row_parts(depth):
    return ((ZO + NZL - depth, ZO - depth, depth), (ZO, ZO + NZL, depth))


def messages():
    table = {}
    for name, buffer, width, first, rows in (
        ("psi", "psi0", 2, 0, XROWS),
        ("eps", "eps", 3, 0, XROWS),
        ("q", "q", 2, 0, XROWS),
        ("n", "n", 1, 0, XROWS),
        ("p", "p", 1, 0, XROWS),
        ("i", "i", 1, 0, XROWS),
        ("psi1", "psi1", 2, 1, EROWS),
        ("psi2", "psi2", 1, 2, EROWS),
    ):
        right, left = x_message(width, first, rows)
        for dx, ((src, dst, count), (lo, hi)) in ((1, right), (-1, left)):
            table.setdefault("x" + name, []).append((buffer, (dx, 0), src, dst, count, lo, lo, hi - lo))
    for name, buffer, depth in (
        ("psi", "psi0", 5),
        ("eps", "eps", 5),
        ("q", "q", 4),
        ("n", "n", 1),
        ("p", "p", 1),
        ("i", "i", 1),
    ):
        for dz, (src, dst, count) in zip((1, -1), row_parts(depth)):
            table.setdefault("z" + name, []).append((buffer, (0, dz), XO, XO, NXL, src, dst, count))
    for name, buffer, width, depth in (("psi", "psi0", 2, 5), ("eps", "eps", 3, 5), ("q", "q", 2, 4)):
        right, left = x_message(width, 0, XROWS)
        for dx, ((xsrc, xdst, xcount), _) in ((1, right), (-1, left)):
            for dz, (src, dst, count) in zip((1, -1), row_parts(depth)):
                table.setdefault("d" + name, []).append((buffer, (dx, dz), xsrc, xdst, xcount, src, dst, count))
    return table


MESSAGES = messages()
INDEX = {}
for _name, _list in MESSAGES.items():
    INDEX[_name] = list(range(sum(map(len, INDEX.values())), sum(map(len, INDEX.values())) + len(_list)))
COUNT = sum(map(len, INDEX.values()))


def blocked(body, first, count, unroll):
    steps = count // unroll
    if steps > 1:

        def step(k, carry):
            for u in range(unroll):
                body(first + k * unroll + u)
            return carry

        lax.fori_loop(0, steps, step, 0)
    else:
        steps = 0
    for u in range(steps * unroll, count):
        body(first + u)


def both_sides(body, first, count, shift):
    def step(side, carry):
        for u in range(count):
            body(first + side * shift + u)
        return carry

    lax.fori_loop(0, 2, step, 0)


def layer_counts(layer_ref):
    kinds = layer_ref[...]

    def total(mask):
        ones = jnp.where(mask, 1.0, 0.0).astype(F32)
        return jnp.sum(jnp.sum(ones, axis=0, keepdims=True), axis=1, keepdims=True)

    return total(kinds == 0), total(kinds <= 1)


def poisson_kernel(
    psi_h, eps_h, n_h, p_h, vac_h, dop_h, layer_ref, height_ref,
    psi4, n_b, p_b, i_b,
    psi0, psi1, psi2, psi3, eps, q, rden, cx, cy, cz, load_sem, send_sem, recv_sem,
):
    gx, gz = lax.axis_index("gx"), lax.axis_index("gz")
    gxs, gzs = lax.axis_size("gx"), lax.axis_size("gz")
    buffers = {"psi0": psi0, "psi1": psi1, "psi2": psi2, "eps": eps, "q": q, "n": n_b, "p": p_b, "i": i_b}

    barrier = pltpu.get_barrier_semaphore()
    for dx in (-1, 0, 1):
        for dz in (-1, 0, 1):
            if dx or dz:
                there = (lax.rem(gx + dx + gxs, gxs), lax.rem(gz + dz + gzs, gzs))
                pl.semaphore_signal(barrier, inc=1, device_id=there, device_id_type=MESH)

    inner = lambda ref: ref.at[pl.ds(XO, NXL), pl.ds(ZO, NZL), :]
    loads = ((eps_h, eps), (psi_h, psi0), (n_h, n_b), (p_h, p_b), (vac_h, i_b), (dop_h, q))
    for k, (source, target) in enumerate(loads):
        for x in range(NXL):
            pltpu.make_async_copy(
                source.at[:, x, :], target.at[XO + x, pl.ds(ZO, NZL), :], load_sem.at[k]
            ).start()

    def loaded(k):
        target = inner(loads[k][1])
        pltpu.make_async_copy(target, target, load_sem.at[k]).wait()

    has = {(0, 0): True}
    has_x = {1: gx < gxs - 1, -1: gx > 0}
    has_z = {1: gz < gzs - 1, -1: gz > 0}

    def exists(direction):
        dx, dz = direction
        if dx == 0:
            return has_z[dz]
        if dz == 0:
            return has_x[dx]
        return jnp.logical_and(has_x[dx], has_z[dz])

    def zero_planes(first):
        for ref in (psi0, eps, q, n_b, p_b, i_b, psi1, psi2):
            for k in range(XO):
                ref[first + k, LO:HI, :] = jnp.zeros((SPAN, NY), F32)

    def zero_rows(first):
        for ref in (psi0, eps, q, n_b, p_b, i_b):
            ref[:, first : first + 8, :] = jnp.zeros((PLANES, 8, NY), F32)

    pl.when(gx == 0)(lambda: zero_planes(0))
    pl.when(gx == gxs - 1)(lambda: zero_planes(XO + NXL))
    pl.when(gz == 0)(lambda: zero_rows(LO))
    pl.when(gz == gzs - 1)(lambda: zero_rows(ZO + NZL))

    def copy_of(name, k):
        buffer, (dx, dz), xs, xd, xc, rs, rd, rc = MESSAGES[name][k]
        ref, at = buffers[buffer], INDEX[name][k]
        return pltpu.make_async_remote_copy(
            src_ref=ref.at[pl.ds(xs, xc), pl.ds(rs, rc), :],
            dst_ref=ref.at[pl.ds(xd, xc), pl.ds(rd, rc), :],
            send_sem=send_sem.at[at],
            recv_sem=recv_sem.at[at],
            device_id=(gx + dx, gz + dz),
            device_id_type=MESH,
        )

    def send(*names):
        for name in names:
            for k, entry in enumerate(MESSAGES[name]):
                pl.when(exists(entry[1]))(lambda name=name, k=k: copy_of(name, k).start())

    def arrived(*names):
        for name in names:
            for k, entry in enumerate(MESSAGES[name]):
                dx, dz = entry[1]
                pl.when(exists((-dx, -dz)))(lambda name=name, k=k: copy_of(name, k).wait_recv())

    def sent(*names):
        for name in names:
            for k, entry in enumerate(MESSAGES[name]):
                pl.when(exists(entry[1]))(lambda name=name, k=k: copy_of(name, k).wait_send())

    loaded(0)
    loaded(1)
    pl.semaphore_wait(barrier, 8)
    send("xpsi", "xeps", "zeps", "zpsi", "dpsi", "deps")

    boundary, _ = layer_counts(layer_ref)
    depth = (lax.broadcasted_iota(jnp.int32, (NZL, NY), 0) + gz * NZL).astype(F32)
    for k in (2, 3, 4, 5):
        loaded(k)

    def charge(x):
        plane = XO + x
        at = (plane, slice(ZO, ZO + NZL))
        level = boundary - height_ref[pl.ds(x, 1), :].astype(F32)
        ions = jnp.where(depth < level, i_b[at], 0.0)
        i_b[at] = ions
        q[at] = 4.0 * (p_b[at] - n_b[at] + ions + q[at])

    blocked(charge, 0, NXL, 2)
    send("zq", "xq", "dq")

    row = lax.broadcasted_iota(jnp.int32, (SPAN, NY), 0)
    above = jnp.where(gz > 0, 0, 8)
    below = jnp.where(gz < gzs - 1, SPAN, SPAN - 8)
    in_z = jnp.logical_and(row >= above, row < below)

    def face_x(plane):
        cx[plane, LO:HI, :] = eps[plane, LO:HI, :] + eps[plane - 1, LO:HI, :]

    def faces(plane):
        mid = eps[plane, LO:HI, :]
        cz[plane, LO:HI, :] = mid + eps[plane, LO - 1 : HI - 1, :]
        cz[plane, HI : HI + 8, :] = eps[plane, HI : HI + 8, :] + eps[plane, HI - 1 : HI + 7, :]
        cy[plane, LO:HI, :] = mid + pltpu.roll(mid, NY - 1, 1)

    def denominator(plane, inside=None):
        side = cy[plane, LO:HI, :]
        total = cx[plane, LO:HI, :] + cx[plane + 1, LO:HI, :] + cz[plane, LO:HI, :]
        total = total + cz[plane, LO + 1 : HI + 1, :] + side + pltpu.roll(side, 1, 1)
        mask = in_z if inside is None else jnp.logical_and(in_z, inside)
        rden[plane, LO:HI, :] = jnp.where(mask, 1.0 / total, 0.0)

    def sweep(source, target):
        def body(plane):
            mid = source[plane, LO:HI, :]
            side = cy[plane, LO:HI, :]
            total = q[plane, LO:HI, :] + cx[plane, LO:HI, :] * source[plane - 1, LO:HI, :]
            total = total + cx[plane + 1, LO:HI, :] * source[plane + 1, LO:HI, :]
            total = total + cz[plane, LO:HI, :] * source[plane, LO - 1 : HI - 1, :]
            total = total + cz[plane, LO + 1 : HI + 1, :] * source[plane, LO + 1 : HI + 1, :]
            total = total + side * pltpu.roll(mid, NY - 1, 1) + pltpu.roll(side * mid, 1, 1)
            target[plane, LO:HI, :] = total * rden[plane, LO:HI, :]

        return body

    arrived("zeps")
    blocked(face_x, XO + 1, NXL - 1, 4)
    blocked(faces, XO, NXL, 4)
    blocked(denominator, XO + 1, NXL - 2, 4)
    arrived("zpsi", "zq")
    both_sides(sweep(psi0, psi1), XO + 1, 2, 12)
    send("xpsi1")
    blocked(sweep(psi0, psi1), XO + 3, 10, 4)
    both_sides(sweep(psi1, psi2), XO + 2, 1, 11)
    send("xpsi2", "xn", "xp", "xi", "zn", "zp", "zi")
    blocked(sweep(psi1, psi2), XO + 3, 10, 4)
    blocked(sweep(psi2, psi3), XO + 3, 10, 4)
    blocked(sweep(psi3, psi4), XO + 4, 8, 4)

    arrived("xeps", "deps")

    def face_x_both(plane):
        face_x(plane)

    both_sides(face_x_both, XO - 2, 3, 18)
    both_sides(faces, XO - 2, 2, 18)

    def denominators(side, carry):
        inside = jnp.where(side == 0, gx > 0, gx < gxs - 1)
        for u in range(3):
            plane = XO - 2 + side * 17 + u
            own = jnp.logical_and(plane >= XO, plane < XO + NXL)
            denominator(plane, jnp.logical_or(own, inside))
        return carry

    lax.fori_loop(0, 2, denominators, 0)
    arrived("xpsi", "dpsi", "xq", "dq")
    both_sides(sweep(psi0, psi1), XO - 1, 2, 16)
    arrived("xpsi1")
    both_sides(sweep(psi1, psi2), XO - 2, 4, 16)
    arrived("xpsi2")
    both_sides(sweep(psi2, psi3), XO - 2, 5, 15)
    both_sides(sweep(psi3, psi4), XO - 1, 5, 13)
    arrived("xn", "xp", "xi", "zn", "zp", "zi")
    sent(*MESSAGES)


def transport_kernel(
    psi, n_b, p_b, i_b, opt_h, layer_ref, height_ref,
    psi_out, n_out, p_out, i_out,
    opt, n_s, p_s, i_s, edge, load_sem, psi_sem, store_sem,
):
    gz = lax.axis_index("gz")
    for x in range(NXL):
        pltpu.make_async_copy(opt_h.at[:, x, :], opt.at[x], load_sem).start()
    for x in range(NXL):
        pltpu.make_async_copy(psi.at[XO + x, pl.ds(ZO, NZL), :], psi_out.at[:, x, :], psi_sem).start()

    boundary, junction = layer_counts(layer_ref)
    depth = (lax.broadcasted_iota(jnp.int32, (NZL, NY), 0) + gz * NZL).astype(F32)

    def flux(a, b):
        u = 0.5 * (b[0] - a[0])
        size = jnp.maximum(jnp.abs(u), TINY)
        mean = size / jnp.tanh(size)
        down, up = mean - u, mean + u
        both = jnp.minimum(a[3], b[3]) > 0.0
        return (
            up * a[1] - down * b[1],
            down * a[2] - up * b[2],
            jnp.where(both, down * a[3] - up * b[3], 0.0),
        )

    fields = (psi, n_b, p_b, i_b)

    def cells(plane, lo, hi):
        return tuple(ref[plane, lo:hi, :] for ref in fields)

    mid = (ZO, ZO + NZL)
    for k, f in enumerate(flux(cells(XO - 1, *mid), cells(XO, *mid))):
        edge[k] = f

    pltpu.make_async_copy(opt, opt, load_sem).wait()

    def plane_of(x):
        plane = XO + x
        here = cells(plane, *mid)
        fx = flux(here, cells(plane + 1, *mid))
        fy = flux(here, tuple(pltpu.roll(f, NY - 1, 1) for f in here))
        fz = flux(cells(plane, ZO - 8, ZO + NZL), cells(plane, ZO - 7, ZO + NZL + 1))
        out = []
        for k in range(3):
            back = pltpu.roll(fz[k], 1, 0)[8:]
            out.append(fx[k] - edge[k] + fy[k] - pltpu.roll(fy[k], 1, 1) + fz[k][8:] - back)
            edge[k] = fx[k]
        _, n, p, i = here
        level = height_ref[pl.ds(x, 1), :].astype(F32)
        rate = jnp.where(depth < boundary - level, 1.0, jnp.where(depth < junction - level, 10.0, 0.2))
        loss = (n * p - 1.0) * rate / (n + p + 2.0)
        gain = 0.05 * (opt[x] - loss)
        n_s[x] = n - 0.04 * out[0] + gain
        p_s[x] = p - 0.03 * out[1] + gain
        i_s[x] = i - 0.02 * out[2]

    def step(x, carry):
        plane_of(x)
        return carry

    lax.fori_loop(0, NXL, step, 0)
    stores = ((n_s, n_out), (p_s, p_out), (i_s, i_out))
    for k, (source, target) in enumerate(stores):
        for x in range(NXL):
            pltpu.make_async_copy(source.at[x], target.at[:, x, :], store_sem.at[k]).start()
    own = psi.at[pl.ds(XO, NXL), pl.ds(ZO, NZL), :]
    pltpu.make_async_copy(own, own, psi_sem).wait()
    for k, (source, target) in enumerate(stores):
        pltpu.make_async_copy(source, source, store_sem.at[k]).wait()


def on_device(psi, n, p, vac, eps, dop, opt, layer, height):
    layer = layer.reshape(8, 128)
    anywhere = pl.BlockSpec(memory_space=pl.ANY)
    near = pl.BlockSpec(memory_space=pltpu.VMEM)
    planes = jax.ShapeDtypeStruct((PLANES, ROWS, NY), F32)
    field = pltpu.VMEM((PLANES, ROWS, NY), F32)
    psi4, n_b, p_b, i_b = pl.pallas_call(
        poisson_kernel,
        out_shape=[planes] * 4,
        in_specs=[anywhere] * 6 + [near] * 2,
        out_specs=[near] * 4,
        scratch_shapes=[field] * 10
        + [
            pltpu.SemaphoreType.DMA((6,)),
            pltpu.SemaphoreType.DMA((COUNT,)),
            pltpu.SemaphoreType.DMA((COUNT,)),
        ],
        compiler_params=pltpu.CompilerParams(
            collective_id=0, has_side_effects=True, vmem_limit_bytes=34 << 20
        ),
        name="poisson",
    )(psi, eps, n, p, vac, dop, layer, height)
    block = jax.ShapeDtypeStruct((NZL, NXL, NY), F32)
    own = pltpu.VMEM((NXL, NZL, NY), F32)
    return pl.pallas_call(
        transport_kernel,
        out_shape=[block] * 4,
        in_specs=[near] * 4 + [anywhere] + [near] * 2,
        out_specs=[anywhere] * 4,
        scratch_shapes=[own] * 4
        + [
            pltpu.VMEM((3, NZL, NY), F32),
            pltpu.SemaphoreType.DMA,
            pltpu.SemaphoreType.DMA,
            pltpu.SemaphoreType.DMA((3,)),
        ],
        compiler_params=pltpu.CompilerParams(vmem_limit_bytes=24 << 20),
        name="transport",
    )(psi4, n_b, p_b, i_b, opt, layer, height)


def solution(mesh):
    grid = P("gz", "gx", None)
    return jax.shard_map(
        on_device,
        mesh=mesh,
        in_specs=(grid,) * 7 + (P(), P("gx", None)),
        out_specs=(grid,) * 4,
        check_vma=False,
    )
```

time: 224 us -> 37.8 us (0.17)
  starting transfers between devices: 130 us -> 0 us
  other arithmetic: 47.1 us -> 0 us
  Pallas kernels: 0 us -> 28 us
  waiting for transfers between devices: 17.9 us -> 0 us
  local copies, waits for them, and re-layouts: 25.2 us -> 8.73 us
    ppermute x38 -> x0, starting transfers between devices: 130 us -> none  [the longest x19 70 us: extended_2(): lax.ppermute(lax.slice_in_dim(block, 0, width, axis=dim), axis, backward)]
    pallas_call x0 -> x2, Pallas kernels: none -> 28 us  [the longest x1 20.8 us: on_device(): pl.pallas_call(poisson_kernel, out_shape=[planes] * 4, in_specs=[anywhere...]
    slice x28 -> x0, local copies, waits for them, and re-layouts: 25.1 us -> none  [the longest x14 10.2 us: neighbours(): jnp.roll(centre, -1, axis=2)]
    add x4 -> x0, other arithmetic: 19.8 us -> none  [the longest x1 11 us: charged_populations(): positive_middle - TIME_STEP * DIFF_HOLE * out_hole]
    ppermute x38 -> x0, waiting for transfers between devices: 17.9 us -> none  [the longest x19 17.7 us: extended_2(): lax.ppermute(lax.slice_in_dim(block, 0, width, axis=dim), axis, backward)]
    div x4 -> x0, other arithmetic: 13.8 us -> none  [sweep(): return numer / denom * (1.0 - outside)]
    sub x1 -> x0, other arithmetic: 9.61 us -> none  [ion_update(): return ion_c - TIME_STEP * DIFF_ION * out_ion]
    unnamed x54 -> x18, local copies, waits for them, and re-layouts: 0.13 us -> 8.73 us
  transfers between devices with their start and end apart: 38 -> 0, of which waited for: 7 -> 0; matrix products, arithmetic and copies ran while one was open for 28% -> 0% of each run, Pallas kernels for 0% -> 0%
where the time goes in v1:
time: 37.8 us; the launch traced here: 37.4 us
  Pallas kernels  28 us (74%)
  local copies, waits for them, and re-layouts  8.73 us (23%)
  between operations  0.67 us (2%)
    pallas_call x1, Pallas kernels, on_device(): pl.pallas_call(poisson_kernel, out_shape=[planes] * 4, in_specs=[anywhere...  20.8 us
    unnamed x18, local copies, waits for them, and re-layouts  8.73 us
    pallas_call x1, Pallas kernels, on_device(): pl.pallas_call(transport_kernel, out_shape=[block] * 4, in_specs=[near] *...  7.23 us

profile of v1, /device:TPU:6, one launch (start us, length us, event | category | flops | bytes accessed | tf_op | source)
XLA Modules:
  0.0 37.4 jit_solution(11010305892842523312)
XLA Ops:
  0.6 0.0 copy-start.1
  0.6 1.2 %copy-done.1 = f32[128,16,128]{2,1,0:T(8,128)S(1)} copy-done((f32[128,16,128]{2,1,0:T(8,128)S(1)}, f32[128,16,128]{2,1,0:T(8,128)}, u32[]{:S(2)}) %copy-start.1) | copy-done | bytes 1048600
  1.9 0.0 copy-start.2
  1.9 1.2 %copy-done.2 = f32[128,16,128]{2,1,0:T(8,128)S(1)} copy-done((f32[128,16,128]{2,1,0:T(8,128)S(1)}, f32[128,16,128]{2,1,0:T(8,128)}, u32[]{:S(2)}) %copy-start.2) | copy-done | bytes 1048600
  3.1 0.0 copy-start.3
  3.1 1.2 %copy-done.3 = f32[128,16,128]{2,1,0:T(8,128)S(1)} copy-done((f32[128,16,128]{2,1,0:T(8,128)S(1)}, f32[128,16,128]{2,1,0:T(8,128)}, u32[]{:S(2)}) %copy-start.3) | copy-done | bytes 1048600
  4.3 0.0 copy-start.4
  4.3 1.2 %copy-done.4 = f32[128,16,128]{2,1,0:T(8,128)S(1)} copy-done((f32[128,16,128]{2,1,0:T(8,128)S(1)}, f32[128,16,128]{2,1,0:T(8,128)}, u32[]{:S(2)}) %copy-start.4) | copy-done | bytes 1048600
  5.5 0.0 copy-start.5
  5.5 1.2 %copy-done.5 = f32[128,16,128]{2,1,0:T(8,128)S(1)} copy-done((f32[128,16,128]{2,1,0:T(8,128)S(1)}, f32[128,16,128]{2,1,0:T(8,128)}, u32[]{:S(2)}) %copy-start.5) | copy-done | bytes 1048600
  6.8 0.0 copy-start.6
  6.8 1.2 %copy-done.6 = f32[128,16,128]{2,1,0:T(8,128)S(1)} copy-done((f32[128,16,128]{2,1,0:T(8,128)S(1)}, f32[128,16,128]{2,1,0:T(8,128)}, u32[]{:S(2)}) %copy-start.6) | copy-done | bytes 1048600
  8.0 0.0 copy-start.7
  8.0 0.7 %copy-done.7 = s32[16,128]{1,0:T(8,128)S(1)} copy-done((s32[16,128]{1,0:T(8,128)S(1)}, s32[16,128]{1,0:T(8,128)}, u32[]{:S(2)}) %copy-start.7) | copy-done | bytes 8216
  8.7 0.0 copy-start.8
  8.7 0.7 %copy-done.8 = s32[1024]{0:T(1024)S(1)} copy-done((s32[1024]{0:T(1024)S(1)}, s32[1024]{0:T(1024)}, u32[]{:S(2)}) %copy-start.8) | copy-done | bytes 4120
  9.4 0.0 copy-start
  9.4 20.8 %poisson.1 = (f32[22,160,128]{2,1,0:T(8,128)S(1)}, f32[22,160,128]{2,1,0:T(8,128)S(1)}, f32[22,160,128]{2,1,0:T(8,128)S(1)}, f32[22,160,128]{2,1,0:T(8,128)S(1)}) custom-call(f32[128,16,128]{2,1,0:T(8,128)S(1)} %copy-done.1, f32[128,16,128]{2,1,0:T(8,128)S(1)} %copy-done.2, f32[128,16,128]{2,1,0:T(8,128)S(1)} %copy-done.3, f32[128,16,128]{2,1,0:T(8,128)S(1)} %copy-done.4, ...), custom_call_target="tpu_custom_call" | custom-call | tf_op jit(solution)/shard_map/poisson/pallas_call | solution.py:373
  30.2 0.0 copy-done
  30.2 7.2 %transport.1 = (f32[128,16,128]{2,1,0:T(8,128)}, f32[128,16,128]{2,1,0:T(8,128)}, f32[128,16,128]{2,1,0:T(8,128)}, f32[128,16,128]{2,1,0:T(8,128)}) custom-call(f32[22,160,128]{2,1,0:T(8,128)S(1)} %get-tuple-element.8.psi, f32[22,160,128]{2,1,0:T(8,128)S(1)} %get-tuple-element.9.n_b, f32[22,160,128]{2,1,0:T(8,128)S(1)} %get-tuple-element.10.p_b, ...), custom_call_target="tpu_custom_call" | custom-call | tf_op jit(solution)/shard_map/transport/pallas_call | solution.py:391
Async XLA Ops:
  0.6 1.2 %copy-start.1 = (f32[128,16,128]{2,1,0:T(8,128)S(1)}, f32[128,16,128]{2,1,0:T(8,128)}, u32[]{:S(2)}) copy-start(f32[128,16,128]{2,1,0:T(8,128)} %psi_h.1) | copy-start | bytes 3145732
  1.9 1.2 %copy-start.2 = (f32[128,16,128]{2,1,0:T(8,128)S(1)}, f32[128,16,128]{2,1,0:T(8,128)}, u32[]{:S(2)}) copy-start(f32[128,16,128]{2,1,0:T(8,128)} %eps_h.1) | copy-start | bytes 3145732
  3.1 1.2 %copy-start.3 = (f32[128,16,128]{2,1,0:T(8,128)S(1)}, f32[128,16,128]{2,1,0:T(8,128)}, u32[]{:S(2)}) copy-start(f32[128,16,128]{2,1,0:T(8,128)} %n_h.1) | copy-start | bytes 3145732
  4.3 1.2 %copy-start.4 = (f32[128,16,128]{2,1,0:T(8,128)S(1)}, f32[128,16,128]{2,1,0:T(8,128)}, u32[]{:S(2)}) copy-start(f32[128,16,128]{2,1,0:T(8,128)} %p_h.1) | copy-start | bytes 3145732
  5.5 1.2 %copy-start.5 = (f32[128,16,128]{2,1,0:T(8,128)S(1)}, f32[128,16,128]{2,1,0:T(8,128)}, u32[]{:S(2)}) copy-start(f32[128,16,128]{2,1,0:T(8,128)} %vac_h.1) | copy-start | bytes 3145732
  6.8 1.2 %copy-start.6 = (f32[128,16,128]{2,1,0:T(8,128)S(1)}, f32[128,16,128]{2,1,0:T(8,128)}, u32[]{:S(2)}) copy-start(f32[128,16,128]{2,1,0:T(8,128)} %dop_h.1) | copy-start | bytes 3145732
  8.0 0.7 %copy-start.7 = (s32[16,128]{1,0:T(8,128)S(1)}, s32[16,128]{1,0:T(8,128)}, u32[]{:S(2)}) copy-start(s32[16,128]{1,0:T(8,128)} %height_ref.3) | copy-start | bytes 24580
  8.7 0.7 %copy-start.8 = (s32[1024]{0:T(1024)S(1)}, s32[1024]{0:T(1024)}, u32[]{:S(2)}) copy-start(s32[1024]{0:T(1024)} %param.16) | copy-start | bytes 12292
  9.4 20.8 %copy-start = (f32[128,16,128]{2,1,0:T(8,128)S(1)}, f32[128,16,128]{2,1,0:T(8,128)}, u32[]{:S(2)}) copy-start(f32[128,16,128]{2,1,0:T(8,128)} %opt_h.1) | copy-start | bytes 3145732

commit v2 on v1

--- a/solution.py
+++ b/solution.py
@@ -21,6 +21,7 @@
 HI = ZO + NZL + 8
 SPAN = HI - LO
 TINY = 1e-10
+STEP = 2
 
 XROWS = (ZO, ZO + NZL)
 EROWS = (LO, HI)
@@ -114,9 +115,10 @@
 
 
 def poisson_kernel(
-    psi_h, eps_h, n_h, p_h, vac_h, dop_h, layer_ref, height_ref,
-    psi4, n_b, p_b, i_b,
-    psi0, psi1, psi2, psi3, eps, q, rden, cx, cy, cz, load_sem, send_sem, recv_sem,
+    psi_h, eps_h, n_h, p_h, vac_h, dop_h, opt_h, layer_h, height_h,
+    psi4, n_b, p_b, i_b, opt,
+    psi0, psi1, psi2, psi3, eps, q, rden, cx, cy, cz, layer_ref, height_ref,
+    load_sem, map_sem, send_sem, recv_sem,
 ):
     gx, gz = lax.axis_index("gx"), lax.axis_index("gz")
     gxs, gzs = lax.axis_size("gx"), lax.axis_size("gz")
@@ -136,6 +138,15 @@
             pltpu.make_async_copy(
                 source.at[:, x, :], target.at[XO + x, pl.ds(ZO, NZL), :], load_sem.at[k]
             ).start()
+
+    maps = (
+        pltpu.make_async_copy(layer_h, layer_ref, map_sem.at[0]),
+        pltpu.make_async_copy(height_h, height_ref, map_sem.at[1]),
+    )
+    for copy in maps:
+        copy.start()
+    for x in range(NXL):
+        pltpu.make_async_copy(opt_h.at[:, x, :], opt.at[x], load_sem.at[6]).start()
 
     def loaded(k):
         target = inner(loads[k][1])
@@ -200,6 +211,8 @@
     pl.semaphore_wait(barrier, 8)
     send("xpsi", "xeps", "zeps", "zpsi", "dpsi", "deps")
 
+    for copy in maps:
+        copy.wait()
     boundary, _ = layer_counts(layer_ref)
     depth = (lax.broadcasted_iota(jnp.int32, (NZL, NY), 0) + gz * NZL).astype(F32)
     for k in (2, 3, 4, 5):
@@ -290,20 +303,24 @@
     both_sides(sweep(psi3, psi4), XO - 1, 5, 13)
     arrived("xn", "xp", "xi", "zn", "zp", "zi")
     sent(*MESSAGES)
+    pltpu.make_async_copy(opt, opt, load_sem.at[6]).wait()
 
 
 def transport_kernel(
-    psi, n_b, p_b, i_b, opt_h, layer_ref, height_ref,
+    psi, n_b, p_b, i_b, opt, layer_h, height_h,
     psi_out, n_out, p_out, i_out,
-    opt, n_s, p_s, i_s, edge, load_sem, psi_sem, store_sem,
+    n_s, p_s, i_s, edge, layer_ref, height_ref, map_sem, psi_sem, store_sem,
 ):
     gz = lax.axis_index("gz")
-    for x in range(NXL):
-        pltpu.make_async_copy(opt_h.at[:, x, :], opt.at[x], load_sem).start()
+    maps = (
+        pltpu.make_async_copy(layer_h, layer_ref, map_sem.at[0]),
+        pltpu.make_async_copy(height_h, height_ref, map_sem.at[1]),
+    )
+    for copy in maps:
+        copy.start()
     for x in range(NXL):
         pltpu.make_async_copy(psi.at[XO + x, pl.ds(ZO, NZL), :], psi_out.at[:, x, :], psi_sem).start()
 
-    boundary, junction = layer_counts(layer_ref)
     depth = (lax.broadcasted_iota(jnp.int32, (NZL, NY), 0) + gz * NZL).astype(F32)
 
     def flux(a, b):
@@ -326,10 +343,12 @@
     mid = (ZO, ZO + NZL)
     for k, f in enumerate(flux(cells(XO - 1, *mid), cells(XO, *mid))):
         edge[k] = f
-
-    pltpu.make_async_copy(opt, opt, load_sem).wait()
-
-    def plane_of(x):
+    for copy in maps:
+        copy.wait()
+    boundary, junction = layer_counts(layer_ref)
+    stores = ((n_s, n_out), (p_s, p_out), (i_s, i_out))
+
+    def plane_of(x, before):
         plane = XO + x
         here = cells(plane, *mid)
         fx = flux(here, cells(plane + 1, *mid))
@@ -338,8 +357,7 @@
         out = []
         for k in range(3):
             back = pltpu.roll(fz[k], 1, 0)[8:]
-            out.append(fx[k] - edge[k] + fy[k] - pltpu.roll(fy[k], 1, 1) + fz[k][8:] - back)
-            edge[k] = fx[k]
+            out.append(fx[k] - before[k] + fy[k] - pltpu.roll(fy[k], 1, 1) + fz[k][8:] - back)
         _, n, p, i = here
         level = height_ref[pl.ds(x, 1), :].astype(F32)
         rate = jnp.where(depth < boundary - level, 1.0, jnp.where(depth < junction - level, 10.0, 0.2))
@@ -348,16 +366,21 @@
         n_s[x] = n - 0.04 * out[0] + gain
         p_s[x] = p - 0.03 * out[1] + gain
         i_s[x] = i - 0.02 * out[2]
-
-    def step(x, carry):
-        plane_of(x)
+        return fx
+
+    def step(k, carry):
+        fx = tuple(edge[m] for m in range(3))
+        for u in range(STEP):
+            fx = plane_of(k * STEP + u, fx)
+        for m in range(3):
+            edge[m] = fx[m]
+        for u in range(STEP):
+            x = k * STEP + u
+            for m, (source, target) in enumerate(stores):
+                pltpu.make_async_copy(source.at[x], target.at[:, x, :], store_sem.at[m]).start()
         return carry
 
-    lax.fori_loop(0, NXL, step, 0)
-    stores = ((n_s, n_out), (p_s, p_out), (i_s, i_out))
-    for k, (source, target) in enumerate(stores):
-        for x in range(NXL):
-            pltpu.make_async_copy(source.at[x], target.at[:, x, :], store_sem.at[k]).start()
+    lax.fori_loop(0, NXL // STEP, step, 0)
     own = psi.at[pl.ds(XO, NXL), pl.ds(ZO, NZL), :]
     pltpu.make_async_copy(own, own, psi_sem).wait()
     for k, (source, target) in enumerate(stores):
@@ -366,18 +389,23 @@
 
 def on_device(psi, n, p, vac, eps, dop, opt, layer, height):
     layer = layer.reshape(8, 128)
-    anywhere = pl.BlockSpec(memory_space=pl.ANY)
+    far = lambda *arrays: [pltpu.with_memory_space_constraint(a, pltpu.HBM) for a in arrays]
+    psi, n, p, vac, eps, dop, opt, layer, height = far(psi, n, p, vac, eps, dop, opt, layer, height)
+    anywhere = pl.BlockSpec(memory_space=pltpu.HBM)
     near = pl.BlockSpec(memory_space=pltpu.VMEM)
+    maps = [pltpu.VMEM((8, 128), jnp.int32), pltpu.VMEM((NXL, NY), jnp.int32)]
     planes = jax.ShapeDtypeStruct((PLANES, ROWS, NY), F32)
     field = pltpu.VMEM((PLANES, ROWS, NY), F32)
-    psi4, n_b, p_b, i_b = pl.pallas_call(
+    psi4, n_b, p_b, i_b, light = pl.pallas_call(
         poisson_kernel,
-        out_shape=[planes] * 4,
-        in_specs=[anywhere] * 6 + [near] * 2,
-        out_specs=[near] * 4,
+        out_shape=[planes] * 4 + [jax.ShapeDtypeStruct((NXL, NZL, NY), F32)],
+        in_specs=[anywhere] * 9,
+        out_specs=[near] * 5,
         scratch_shapes=[field] * 10
+        + maps
         + [
-            pltpu.SemaphoreType.DMA((6,)),
+            pltpu.SemaphoreType.DMA((7,)),
+            pltpu.SemaphoreType.DMA((2,)),
             pltpu.SemaphoreType.DMA((COUNT,)),
             pltpu.SemaphoreType.DMA((COUNT,)),
         ],
@@ -385,24 +413,25 @@
             collective_id=0, has_side_effects=True, vmem_limit_bytes=34 << 20
         ),
         name="poisson",
-    )(psi, eps, n, p, vac, dop, layer, height)
+    )(psi, eps, n, p, vac, dop, opt, layer, height)
     block = jax.ShapeDtypeStruct((NZL, NXL, NY), F32)
     own = pltpu.VMEM((NXL, NZL, NY), F32)
     return pl.pallas_call(
         transport_kernel,
         out_shape=[block] * 4,
-        in_specs=[near] * 4 + [anywhere] + [near] * 2,
+        in_specs=[near] * 5 + [anywhere] * 2,
         out_specs=[anywhere] * 4,
-        scratch_shapes=[own] * 4
+        scratch_shapes=[own] * 3
         + [
             pltpu.VMEM((3, NZL, NY), F32),
-            pltpu.SemaphoreType.DMA,
+            *maps,
+            pltpu.SemaphoreType.DMA((2,)),
             pltpu.SemaphoreType.DMA,
             pltpu.SemaphoreType.DMA((3,)),
         ],
         compiler_params=pltpu.CompilerParams(vmem_limit_bytes=24 << 20),
         name="transport",
-    )(psi4, n_b, p_b, i_b, opt, layer, height)
+    )(psi4, n_b, p_b, i_b, light, layer, height)
 
 
 def solution(mesh):

time: 37.8 us -> 27.4 us (0.72)
  local copies, waits for them, and re-layouts: 8.73 us -> 0 us
  Pallas kernels: 28 us -> 26.6 us
    unnamed x18 -> x0, local copies, waits for them, and re-layouts: 8.73 us -> none
    pallas_call x1, Pallas kernels: 7.23 us -> 5.77 us  [on_device(): pl.pallas_call(transport_kernel, out_shape=[block] * 4, in_specs=[near] *...]
where the time goes in v2:
time: 27.4 us; the launch traced here: 27.3 us
  Pallas kernels  26.6 us (97%)
  between operations  0.64 us (2%)
    pallas_call x1, Pallas kernels, on_device(): pl.pallas_call(poisson_kernel, out_shape=[planes] * 4 + [jax.ShapeDtypeSt...  20.8 us
    pallas_call x1, Pallas kernels, on_device(): pl.pallas_call(transport_kernel, out_shape=[block] * 4, in_specs=[near] *...  5.77 us

profile of v2, /device:TPU:6, one launch (start us, length us, event | category | flops | bytes accessed | tf_op | source)
XLA Modules:
  0.0 27.3 jit_solution(1586018998549988931)
XLA Ops:
  0.6 20.8 %poisson.1 = (f32[22,160,128]{2,1,0:T(8,128)S(1)}, f32[22,160,128]{2,1,0:T(8,128)S(1)}, f32[22,160,128]{2,1,0:T(8,128)S(1)}, f32[22,160,128]{2,1,0:T(8,128)S(1)}, f32[16,128,128]{2,1,0:T(8,128)S(1)}) custom-call(f32[128,16,128]{2,1,0:T(8,128)} %psi_h.1, f32[128,16,128]{2,1,0:T(8,128)} %eps_h.1, f32[128,16,128]{2,1,0:T(8,128)} %n_h.1, f32[128,16,128]{2,1,0:T(8,128)} %p_h.1, ...), custom_call_target="tpu_custom_call" | custom-call | tf_op jit(solution)/shard_map/poisson/pallas_call | solution.py:399
  21.5 5.8 %transport.1 = (f32[128,16,128]{2,1,0:T(8,128)}, f32[128,16,128]{2,1,0:T(8,128)}, f32[128,16,128]{2,1,0:T(8,128)}, f32[128,16,128]{2,1,0:T(8,128)}) custom-call(f32[22,160,128]{2,1,0:T(8,128)S(1)} %get-tuple-element.9.psi, f32[22,160,128]{2,1,0:T(8,128)S(1)} %get-tuple-element.10.n_b, f32[22,160,128]{2,1,0:T(8,128)S(1)} %get-tuple-element.11.p_b, ...), custom_call_target="tpu_custom_call" | custom-call | tf_op jit(solution)/shard_map/transport/pallas_call | solution.py:419

commit v3 on v2

v3 whole, which is shorter than its diff:
```python
import functools

import jax
import jax.numpy as jnp
from jax import lax
from jax.experimental import pallas as pl
from jax.experimental.pallas import tpu as pltpu
from jax.sharding import PartitionSpec as P

MESH = pl.DeviceIdType.MESH
F32 = jnp.float32

NXL = 16
NZL = 128
NY = 128
XO = 3
ZO = 16
PLANES = NXL + 2 * XO
ROWS = NZL + 2 * ZO
LO = ZO - 8
HI = ZO + NZL + 8
SPAN = HI - LO
TINY = 1e-10
EARLY = 5
DONE = 6

XROWS = (ZO, ZO + NZL)


def x_message(width, first, rows):
    low = XO - first - width
    return (
        ((XO + NXL - first - width, low, width), rows),
        ((XO + first, XO + NXL + first, width), rows),
    )


def row_parts(depth):
    return ((ZO + NZL - depth, ZO - depth, depth), (ZO, ZO + NZL, depth))


def messages():
    table = {}
    for name, buffer, width, first, rows in (
        ("psi", "psi0", 2, 0, XROWS),
        ("eps", "eps", 2, 0, XROWS),
        ("q", "q", 1, 0, XROWS),
        ("n", "n", 1, 0, XROWS),
        ("p", "p", 1, 0, XROWS),
        ("i", "i", 1, 0, XROWS),
        ("psi1", "psi1", 1, 1, (ZO - 3, ZO + NZL + 3)),
        ("rden", "rden", 1, 1, (ZO - 2, ZO + NZL + 2)),
    ):
        right, left = x_message(width, first, rows)
        for dx, ((src, dst, count), (lo, hi)) in ((1, right), (-1, left)):
            table.setdefault("x" + name, []).append((buffer, (dx, 0), src, dst, count, lo, lo, hi - lo))
    for name, level, depth in (("part1", 0, 2), ("part2", 1, 1)):
        for dx, side in ((1, 0), (-1, 1)):
            rows = (ZO - depth, ZO - depth, NZL + 2 * depth)
            table.setdefault("x" + name, []).append(("part", (dx, 0), 2 * side + level, 4 + 2 * side + level, 1) + rows)
    for name, buffer, depth in (
        ("psi", "psi0", 5),
        ("eps", "eps", 5),
        ("q", "q", 4),
        ("n", "n", 1),
        ("p", "p", 1),
        ("i", "i", 1),
    ):
        for dz, (src, dst, count) in zip((1, -1), row_parts(depth)):
            table.setdefault("z" + name, []).append((buffer, (0, dz), XO, XO, NXL, src, dst, count))
    for name, buffer, width, depth in (("psi", "psi0", 2, 5), ("eps", "eps", 2, 5), ("q", "q", 1, 4)):
        right, left = x_message(width, 0, XROWS)
        for dx, ((xsrc, xdst, xcount), _) in ((1, right), (-1, left)):
            for dz, (src, dst, count) in zip((1, -1), row_parts(depth)):
                table.setdefault("d" + name, []).append((buffer, (dx, dz), xsrc, xdst, xcount, src, dst, count))
    return table


MESSAGES = messages()
INDEX = {}
for _name, _list in MESSAGES.items():
    INDEX[_name] = list(range(sum(map(len, INDEX.values())), sum(map(len, INDEX.values())) + len(_list)))
COUNT = sum(map(len, INDEX.values()))


def blocked(body, first, count, unroll):
    steps = count // unroll
    if steps > 1:

        def step(k, carry):
            for u in range(unroll):
                body(first + k * unroll + u)
            return carry

        lax.fori_loop(0, steps, step, 0)
    else:
        steps = 0
    for u in range(steps * unroll, count):
        body(first + u)


def both_sides(body, first, count, shift):
    def step(side, carry):
        for u in range(count):
            body(first + side * shift + u)
        return carry

    lax.fori_loop(0, 2, step, 0)


def layer_counts(layer_ref):
    kinds = layer_ref[...]

    def total(mask):
        ones = jnp.where(mask, 1.0, 0.0).astype(F32)
        return jnp.sum(jnp.sum(ones, axis=0, keepdims=True), axis=1, keepdims=True)

    return total(kinds == 0), total(kinds <= 1)


def poisson_kernel(
    psi_h, eps_h, n_h, p_h, vac_h, dop_h, opt_h, layer_h, height_h,
    psi4, n_b, p_b, i_b, opt, n_s, p_s, i_s,
    psi0, psi1, psi2, psi3, eps, q, rden, cx, cy, cz, part, layer_ref, height_ref,
    load_sem, map_sem, send_sem, recv_sem,
):
    gx, gz = lax.axis_index("gx"), lax.axis_index("gz")
    gxs, gzs = lax.axis_size("gx"), lax.axis_size("gz")
    buffers = {"psi0": psi0, "psi1": psi1, "rden": rden, "part": part, "eps": eps, "q": q, "n": n_b, "p": p_b, "i": i_b}

    has_x = {1: gx < gxs - 1, -1: gx > 0}
    has_z = {1: gz < gzs - 1, -1: gz > 0}

    def exists(direction):
        dx, dz = direction
        if dx == 0:
            return has_z[dz]
        if dz == 0:
            return has_x[dx]
        return jnp.logical_and(has_x[dx], has_z[dz])

    barrier = pltpu.get_barrier_semaphore()
    for dx in (-1, 0, 1):
        for dz in (-1, 0, 1):
            if dx or dz:

                @pl.when(exists((dx, dz)))
                def _(there=(gx + dx, gz + dz)):
                    pl.semaphore_signal(barrier, inc=1, device_id=there, device_id_type=MESH)

    one = lambda flag: jnp.where(flag, 1, 0)
    columns = 1 + one(has_x[1]) + one(has_x[-1])
    beside = columns * (1 + one(has_z[1]) + one(has_z[-1])) - 1

    inner = lambda ref: ref.at[pl.ds(XO, NXL), pl.ds(ZO, NZL), :]
    loads = ((eps_h, eps), (psi_h, psi0), (n_h, n_b), (p_h, p_b), (vac_h, i_b), (dop_h, q))
    for k, (source, target) in enumerate(loads):
        for x in range(NXL):
            pltpu.make_async_copy(
                source.at[:, x, :], target.at[XO + x, pl.ds(ZO, NZL), :], load_sem.at[k]
            ).start()

    maps = (
        pltpu.make_async_copy(layer_h, layer_ref, map_sem.at[0]),
        pltpu.make_async_copy(height_h, height_ref, map_sem.at[1]),
    )
    for copy in maps:
        copy.start()
    for x in range(NXL):
        pltpu.make_async_copy(opt_h.at[:, x, :], opt.at[x], load_sem.at[6]).start()

    def loaded(k):
        target = inner(loads[k][1])
        pltpu.make_async_copy(target, target, load_sem.at[k]).wait()

    def zero_planes(first):
        for ref in (psi0, eps, q, n_b, p_b, i_b, psi1, rden):
            for k in range(XO):
                ref[first + k, LO:HI, :] = jnp.zeros((SPAN, NY), F32)
        for k in range(2):
            part[(4 if first == 0 else 6) + k, LO:HI, :] = jnp.zeros((SPAN, NY), F32)

    def zero_rows(first):
        for ref in (psi0, eps, q, n_b, p_b, i_b):
            ref[:, first : first + 8, :] = jnp.zeros((PLANES, 8, NY), F32)

    pl.when(gx == 0)(lambda: zero_planes(0))
    pl.when(gx == gxs - 1)(lambda: zero_planes(XO + NXL))
    pl.when(gz == 0)(lambda: zero_rows(LO))
    pl.when(gz == gzs - 1)(lambda: zero_rows(ZO + NZL))

    def copy_of(name, k):
        buffer, (dx, dz), xs, xd, xc, rs, rd, rc = MESSAGES[name][k]
        ref, at = buffers[buffer], INDEX[name][k]
        return pltpu.make_async_remote_copy(
            src_ref=ref.at[pl.ds(xs, xc), pl.ds(rs, rc), :],
            dst_ref=ref.at[pl.ds(xd, xc), pl.ds(rd, rc), :],
            send_sem=send_sem.at[at],
            recv_sem=recv_sem.at[at],
            device_id=(gx + dx, gz + dz),
            device_id_type=MESH,
        )

    def send(*names):
        for name in names:
            for k, entry in enumerate(MESSAGES[name]):
                pl.when(exists(entry[1]))(lambda name=name, k=k: copy_of(name, k).start())

    def arrived(*names):
        for name in names:
            for k, entry in enumerate(MESSAGES[name]):
                dx, dz = entry[1]
                pl.when(exists((-dx, -dz)))(lambda name=name, k=k: copy_of(name, k).wait_recv())

    def sent(*names):
        for name in names:
            for k, entry in enumerate(MESSAGES[name]):
                pl.when(exists(entry[1]))(lambda name=name, k=k: copy_of(name, k).wait_send())

    row = lax.broadcasted_iota(jnp.int32, (SPAN, NY), 0) + LO
    above = jnp.where(gz > 0, LO, ZO)
    below = jnp.where(gz < gzs - 1, HI, ZO + NZL)
    in_z = jnp.logical_and(row >= above, row < below)

    def face_x(plane, lo, hi):
        cx[plane, lo:hi, :] = eps[plane, lo:hi, :] + eps[plane - 1, lo:hi, :]

    def faces(plane, lo, hi):
        mid = eps[plane, lo:hi, :]
        cz[plane, lo:hi, :] = mid + eps[plane, lo - 1 : hi - 1, :]
        if hi == HI:
            cz[plane, HI : HI + 8, :] = eps[plane, HI : HI + 8, :] + eps[plane, HI - 1 : HI + 7, :]
        cy[plane, lo:hi, :] = mid + pltpu.roll(mid, NY - 1, 1)

    def denominator(plane, lo, hi, inside=None):
        side = cy[plane, lo:hi, :]
        total = cx[plane, lo:hi, :] + cx[plane + 1, lo:hi, :] + cz[plane, lo:hi, :]
        total = total + cz[plane, lo + 1 : hi + 1, :] + side + pltpu.roll(side, 1, 1)
        mask = in_z[lo - LO : hi - LO]
        if inside is not None:
            mask = jnp.logical_and(mask, inside)
        rden[plane, lo:hi, :] = jnp.where(mask, 1.0 / total, 0.0)

    def sweep(source, target, skip=None, partial=None):
        def body(plane):
            mid = source[plane, LO:HI, :]
            side = cy[plane, LO:HI, :]
            total = q[plane, LO:HI, :] if partial is None else part[partial, LO:HI, :]
            if skip != -1:
                total = total + cx[plane, LO:HI, :] * source[plane - 1, LO:HI, :]
            if skip != 1:
                total = total + cx[plane + 1, LO:HI, :] * source[plane + 1, LO:HI, :]
            total = total + cz[plane, LO:HI, :] * source[plane, LO - 1 : HI - 1, :]
            total = total + cz[plane, LO + 1 : HI + 1, :] * source[plane, LO + 1 : HI + 1, :]
            total = total + side * pltpu.roll(mid, NY - 1, 1) + pltpu.roll(side * mid, 1, 1)
            target[plane, LO:HI, :] = total * rden[plane, LO:HI, :]

        return body

    def partial_sums(level, source):
        for side, plane, face, beyond in ((0, XO + NXL - 2, XO + NXL - 2, XO + NXL - 3), (1, XO + 1, XO + 2, XO + 2)):
            part[2 * side + level, LO:HI, :] = (
                q[plane, LO:HI, :] + cx[face, LO:HI, :] * source[beyond, LO:HI, :]
            )

    loaded(0)
    loaded(1)
    pl.semaphore_wait(barrier, beside)
    send("zeps", "zpsi", "xpsi", "xeps", "dpsi", "deps")

    first, last = ZO + 8, ZO + NZL - 8
    blocked(lambda plane: face_x(plane, *MID), XO + 1, NXL - 1, 4)
    blocked(lambda plane: faces(plane, first, ZO + NZL), XO, NXL, 4)
    blocked(lambda plane: denominator(plane, first, last), XO + 1, NXL - 2, 4)

    loaded(2)
    loaded(3)
    send("xn", "xp")
    for copy in maps:
        copy.wait()
    boundary, junction = layer_counts(layer_ref)
    depth = (lax.broadcasted_iota(jnp.int32, (NZL, NY), 0) + gz * NZL).astype(F32)
    loaded(4)
    loaded(5)

    def charge(x):
        plane = XO + x
        at = (plane, slice(ZO, ZO + NZL))
        level = boundary - height_ref[pl.ds(x, 1), :].astype(F32)
        ions = jnp.where(depth < level, i_b[at], 0.0)
        i_b[at] = ions
        q[at] = 4.0 * (p_b[at] - n_b[at] + ions + q[at])

    blocked(charge, 0, NXL, 2)
    send("zq", "xq", "dq", "zn", "zp", "zi")

    arrived("zeps")

    def rim(body, low, high):
        def both(plane):
            body(plane, LO, low)
            body(plane, high, HI)

        return both

    blocked(rim(face_x, ZO, ZO + NZL), XO + 1, NXL - 1, 4)
    blocked(rim(faces, first, ZO + NZL), XO, NXL, 4)
    blocked(rim(denominator, first, last), XO + 1, NXL - 2, 4)
    send("xrden")
    arrived("zpsi", "zq")
    both_sides(sweep(psi0, psi1), XO + 1, 2, 12)
    partial_sums(0, psi1)
    send("xpsi1", "xpart1")
    both_sides(sweep(psi0, psi1), XO + 3, 1, 9)
    both_sides(sweep(psi1, psi2), XO + 2, 1, 11)
    partial_sums(1, psi2)
    send("xpart2", "xi")
    blocked(sweep(psi0, psi1), XO + 4, 8, 4)
    blocked(sweep(psi1, psi2), XO + 3, 10, 4)
    blocked(sweep(psi2, psi3), XO + 3, 10, 4)
    blocked(sweep(psi3, psi4), XO + 4, 8, 4)

    pltpu.make_async_copy(opt, opt, load_sem.at[6]).wait()
    arrived("zn", "zp", "zi")
    fields = (psi4, n_b, p_b, i_b)
    update = updater(fields, opt, height_ref, boundary, junction, depth)

    def finish(k, flow):
        for u in range(2):
            flow, result = update(EARLY + 2 * k + u, flow)
            for ref, value in zip((n_s, p_s, i_s), result):
                ref[2 * k + u] = value
        return flow

    lax.fori_loop(0, DONE // 2, finish, face_flow(fields, EARLY))

    arrived("xeps", "deps")
    both_sides(lambda plane: face_x(plane, LO, HI), XO - 1, 2, 17)
    both_sides(lambda plane: faces(plane, LO, HI), XO - 2, 2, 18)

    def denominators(side, carry):
        inside = jnp.where(side == 0, gx > 0, gx < gxs - 1)
        for u in range(2):
            plane = XO - 1 + side * 16 + u
            own = jnp.logical_and(plane >= XO, plane < XO + NXL)
            denominator(plane, LO, HI, jnp.logical_or(own, inside))
        return carry

    lax.fori_loop(0, 2, denominators, 0)
    arrived("xpsi", "dpsi", "xq", "dq")
    both_sides(sweep(psi0, psi1), XO - 1, 2, 16)
    arrived("xrden", "xpsi1", "xpart1")
    both_sides(sweep(psi1, psi2), XO - 1, 3, 15)
    sweep(psi1, psi2, -1, 4)(XO - 2)
    sweep(psi1, psi2, 1, 6)(XO + NXL + 1)
    arrived("xpart2")
    both_sides(sweep(psi2, psi3), XO - 1, 4, 14)
    sweep(psi2, psi3, -1, 5)(XO - 2)
    sweep(psi2, psi3, 1, 7)(XO + NXL + 1)
    both_sides(sweep(psi3, psi4), XO - 1, 5, 13)
    arrived("xn", "xp", "xi")
    sent(*MESSAGES)


def flux(a, b):
    u = 0.5 * (b[0] - a[0])
    size = jnp.maximum(jnp.abs(u), TINY)
    mean = size / jnp.tanh(size)
    down, up = mean - u, mean + u
    both = jnp.minimum(a[3], b[3]) > 0.0
    return (
        up * a[1] - down * b[1],
        down * a[2] - up * b[2],
        jnp.where(both, down * a[3] - up * b[3], 0.0),
    )


def cells(fields, plane, lo, hi):
    return tuple(ref[plane, lo:hi, :] for ref in fields)


MID = (ZO, ZO + NZL)


def face_flow(fields, x):
    return flux(cells(fields, XO + x - 1, *MID), cells(fields, XO + x, *MID))


def updater(fields, opt, height_ref, boundary, junction, depth):
    def update(x, before):
        plane = XO + x
        here = cells(fields, plane, *MID)
        fx = flux(here, cells(fields, plane + 1, *MID))
        fy = flux(here, tuple(pltpu.roll(f, NY - 1, 1) for f in here))
        fz = flux(cells(fields, plane, ZO - 8, ZO + NZL), cells(fields, plane, ZO - 7, ZO + NZL + 1))
        out = []
        for k in range(3):
            back = pltpu.roll(fz[k], 1, 0)[8:]
            out.append(fx[k] - before[k] + fy[k] - pltpu.roll(fy[k], 1, 1) + fz[k][8:] - back)
        _, n, p, i = here
        level = height_ref[pl.ds(x, 1), :].astype(F32)
        rate = jnp.where(depth < boundary - level, 1.0, jnp.where(depth < junction - level, 10.0, 0.2))
        loss = (n * p - 1.0) * rate / (n + p + 2.0)
        gain = 0.05 * (opt[x] - loss)
        return fx, (n - 0.04 * out[0] + gain, p - 0.03 * out[1] + gain, i - 0.02 * out[2])

    return update


def transport_kernel(
    psi, n_b, p_b, i_b, opt, n_d, p_d, i_d, layer_h, height_h,
    psi_out, n_out, p_out, i_out,
    n_s, p_s, i_s, layer_ref, height_ref, map_sem, psi_sem, store_sem,
):
    gz = lax.axis_index("gz")
    maps = (
        pltpu.make_async_copy(layer_h, layer_ref, map_sem.at[0]),
        pltpu.make_async_copy(height_h, height_ref, map_sem.at[1]),
    )
    for copy in maps:
        copy.start()
    for x in range(NXL):
        pltpu.make_async_copy(psi.at[XO + x, pl.ds(ZO, NZL), :], psi_out.at[:, x, :], psi_sem).start()
    stores = ((n_s, n_d, n_out), (p_s, p_d, p_out), (i_s, i_d, i_out))
    for m, (_, done, target) in enumerate(stores):
        for k in range(DONE):
            pltpu.make_async_copy(done.at[k], target.at[:, EARLY + k, :], store_sem.at[m]).start()

    depth = (lax.broadcasted_iota(jnp.int32, (NZL, NY), 0) + gz * NZL).astype(F32)
    fields = (psi, n_b, p_b, i_b)
    for copy in maps:
        copy.wait()
    boundary, junction = layer_counts(layer_ref)
    update = updater(fields, opt, height_ref, boundary, junction, depth)

    def step(side, carry):
        first = side * (EARLY + DONE)
        flow = face_flow(fields, first)
        for u in range(EARLY):
            x = first + u
            flow, result = update(x, flow)
            for m, (source, _, target) in enumerate(stores):
                source[x] = result[m]
                pltpu.make_async_copy(source.at[x], target.at[:, x, :], store_sem.at[m]).start()
        return carry

    lax.fori_loop(0, 2, step, 0)
    own = psi.at[pl.ds(XO, NXL), pl.ds(ZO, NZL), :]
    pltpu.make_async_copy(own, own, psi_sem).wait()
    for k, (source, _, target) in enumerate(stores):
        pltpu.make_async_copy(source, source, store_sem.at[k]).wait()


def on_device(psi, n, p, vac, eps, dop, opt, layer, height):
    layer = layer.reshape(8, 128)
    far = lambda *arrays: [pltpu.with_memory_space_constraint(a, pltpu.HBM) for a in arrays]
    psi, n, p, vac, eps, dop, opt, layer, height = far(psi, n, p, vac, eps, dop, opt, layer, height)
    anywhere = pl.BlockSpec(memory_space=pltpu.HBM)
    near = pl.BlockSpec(memory_space=pltpu.VMEM)
    maps = [pltpu.VMEM((8, 128), jnp.int32), pltpu.VMEM((NXL, NY), jnp.int32)]
    planes = jax.ShapeDtypeStruct((PLANES, ROWS, NY), F32)
    field = pltpu.VMEM((PLANES, ROWS, NY), F32)
    psi4, n_b, p_b, i_b, light, *done = pl.pallas_call(
        poisson_kernel,
        out_shape=[planes] * 4
        + [jax.ShapeDtypeStruct((NXL, NZL, NY), F32)]
        + [jax.ShapeDtypeStruct((DONE, NZL, NY), F32)] * 3,
        in_specs=[anywhere] * 9,
        out_specs=[near] * 8,
        scratch_shapes=[field] * 10
        + [pltpu.VMEM((8, ROWS, NY), F32)]
        + maps
        + [
            pltpu.SemaphoreType.DMA((7,)),
            pltpu.SemaphoreType.DMA((2,)),
            pltpu.SemaphoreType.DMA((COUNT,)),
            pltpu.SemaphoreType.DMA((COUNT,)),
        ],
        compiler_params=pltpu.CompilerParams(
            collective_id=0, has_side_effects=True, vmem_limit_bytes=34 << 20
        ),
        name="poisson",
    )(psi, eps, n, p, vac, dop, opt, layer, height)
    block = jax.ShapeDtypeStruct((NZL, NXL, NY), F32)
    own = pltpu.VMEM((NXL, NZL, NY), F32)
    return pl.pallas_call(
        transport_kernel,
        out_shape=[block] * 4,
        in_specs=[near] * 8 + [anywhere] * 2,
        out_specs=[anywhere] * 4,
        scratch_shapes=[own] * 3
        + [
            *maps,
            pltpu.SemaphoreType.DMA((2,)),
            pltpu.SemaphoreType.DMA,
            pltpu.SemaphoreType.DMA((3,)),
        ],
        compiler_params=pltpu.CompilerParams(vmem_limit_bytes=24 << 20),
        name="transport",
    )(psi4, n_b, p_b, i_b, light, *done, layer, height)


def solution(mesh):
    grid = P("gz", "gx", None)
    return jax.shard_map(
        on_device,
        mesh=mesh,
        in_specs=(grid,) * 7 + (P(), P("gx", None)),
        out_specs=(grid,) * 4,
        check_vma=False,
    )
```

time: 27.4 us -> 23.7 us (0.86)
  the two profiles are of different devices: /device:TPU:6 before, /device:TPU:70 now
where the time goes in v3:
time: 23.7 us; the launch traced here: 23.6 us
  Pallas kernels  22.9 us (97%)
  between operations  0.64 us (3%)
    pallas_call x1, Pallas kernels, on_device(): pl.pallas_call(poisson_kernel, out_shape=[planes] * 4 + [jax.ShapeDtypeSt...  18.8 us
    pallas_call x1, Pallas kernels, on_device(): pl.pallas_call(transport_kernel, out_shape=[block] * 4, in_specs=[near] *...  4.17 us

profile of v3, /device:TPU:70, one launch (start us, length us, event | category | flops | bytes accessed | tf_op | source)
XLA Modules:
  0.0 23.6 jit_solution(14406083534691123042)
XLA Ops:
  0.6 18.8 %poisson.1 = (f32[22,160,128]{2,1,0:T(8,128)S(1)}, f32[22,160,128]{2,1,0:T(8,128)S(1)}, f32[22,160,128]{2,1,0:T(8,128)S(1)}, f32[22,160,128]{2,1,0:T(8,128)S(1)}...) custom-call(f32[128,16,128]{2,1,0:T(8,128)} %psi_h.1, ...), custom_call_target="tpu_custom_call" | custom-call | tf_op jit(solution)/shard_map/poisson/pallas_call | solution.py:463
  19.4 4.2 %transport.1 = (f32[128,16,128]{2,1,0:T(8,128)}, f32[128,16,128]{2,1,0:T(8,128)}, f32[128,16,128]{2,1,0:T(8,128)}, f32[128,16,128]{2,1,0:T(8,128)}) custom-call(f32[22,160,128]{2,1,0:T(8,128)S(1)} %get-tuple-element.12.psi, f32[22,160,128]{2,1,0:T(8,128)S(1)} %get-tuple-element.13.n_b, f32[22,160,128]{2,1,0:T(8,128)S(1)} %get-tuple-element.14.p_b, ...), custom_call_target="tpu_custom_call" | custom-call | tf_op jit(solution)/shard_map/transport/pallas_call | solution.py:486

commit v4 on v3

--- a/solution.py
+++ b/solution.py
@@ -21,8 +21,7 @@
 HI = ZO + NZL + 8
 SPAN = HI - LO
 TINY = 1e-10
-EARLY = 5
-DONE = 6
+DONE = 8
 
 XROWS = (ZO, ZO + NZL)
 
@@ -71,8 +70,8 @@
     for name, buffer, width, depth in (("psi", "psi0", 2, 5), ("eps", "eps", 2, 5), ("q", "q", 1, 4)):
         right, left = x_message(width, 0, XROWS)
         for dx, ((xsrc, xdst, xcount), _) in ((1, right), (-1, left)):
-            for dz, (src, dst, count) in zip((1, -1), row_parts(depth)):
-                table.setdefault("d" + name, []).append((buffer, (dx, dz), xsrc, xdst, xcount, src, dst, count))
+            for dz, first in ((-1, ZO - depth), (1, ZO + NZL)):
+                table.setdefault("c" + name, []).append((buffer, (dx, 0), xsrc, xdst, xcount, first, first, depth, dz))
     return table
 
 
@@ -131,26 +130,18 @@
     has_x = {1: gx < gxs - 1, -1: gx > 0}
     has_z = {1: gz < gzs - 1, -1: gz > 0}
 
-    def exists(direction):
-        dx, dz = direction
-        if dx == 0:
-            return has_z[dz]
-        if dz == 0:
-            return has_x[dx]
-        return jnp.logical_and(has_x[dx], has_z[dz])
+    def exists(dx, dz):
+        return has_x[dx] if dx else has_z[dz]
 
     barrier = pltpu.get_barrier_semaphore()
-    for dx in (-1, 0, 1):
-        for dz in (-1, 0, 1):
-            if dx or dz:
-
-                @pl.when(exists((dx, dz)))
-                def _(there=(gx + dx, gz + dz)):
-                    pl.semaphore_signal(barrier, inc=1, device_id=there, device_id_type=MESH)
+    for dx, dz in ((-1, 0), (1, 0), (0, -1), (0, 1)):
+
+        @pl.when(exists(dx, dz))
+        def _(there=(gx + dx, gz + dz)):
+            pl.semaphore_signal(barrier, inc=1, device_id=there, device_id_type=MESH)
 
     one = lambda flag: jnp.where(flag, 1, 0)
-    columns = 1 + one(has_x[1]) + one(has_x[-1])
-    beside = columns * (1 + one(has_z[1]) + one(has_z[-1])) - 1
+    beside = one(has_x[1]) + one(has_x[-1]) + one(has_z[1]) + one(has_z[-1])
 
     inner = lambda ref: ref.at[pl.ds(XO, NXL), pl.ds(ZO, NZL), :]
     loads = ((eps_h, eps), (psi_h, psi0), (n_h, n_b), (p_h, p_b), (vac_h, i_b), (dop_h, q))
@@ -190,7 +181,7 @@
     pl.when(gz == gzs - 1)(lambda: zero_rows(ZO + NZL))
 
     def copy_of(name, k):
-        buffer, (dx, dz), xs, xd, xc, rs, rd, rc = MESSAGES[name][k]
+        buffer, (dx, dz), xs, xd, xc, rs, rd, rc = MESSAGES[name][k][:8]
         ref, at = buffers[buffer], INDEX[name][k]
         return pltpu.make_async_remote_copy(
             src_ref=ref.at[pl.ds(xs, xc), pl.ds(rs, rc), :],
@@ -201,21 +192,29 @@
             device_id_type=MESH,
         )
 
+    def when(entry, sender, action, side=None):
+        dx, dz = entry[1] if sender else (-entry[1][0], -entry[1][1])
+        flag = exists(dx, dz)
+        if len(entry) > 8:
+            flag = jnp.logical_and(flag, has_z[entry[8]])
+        if side is not None:
+            flag = jnp.logical_and(flag, side == (0 if dx < 0 else 1))
+        pl.when(flag)(action)
+
     def send(*names):
         for name in names:
             for k, entry in enumerate(MESSAGES[name]):
-                pl.when(exists(entry[1]))(lambda name=name, k=k: copy_of(name, k).start())
-
-    def arrived(*names):
+                when(entry, True, lambda name=name, k=k: copy_of(name, k).start())
+
+    def arrived(*names, side=None):
         for name in names:
             for k, entry in enumerate(MESSAGES[name]):
-                dx, dz = entry[1]
-                pl.when(exists((-dx, -dz)))(lambda name=name, k=k: copy_of(name, k).wait_recv())
+                when(entry, False, lambda name=name, k=k: copy_of(name, k).wait_recv(), side)
 
     def sent(*names):
         for name in names:
             for k, entry in enumerate(MESSAGES[name]):
-                pl.when(exists(entry[1]))(lambda name=name, k=k: copy_of(name, k).wait_send())
+                when(entry, True, lambda name=name, k=k: copy_of(name, k).wait_send())
 
     row = lax.broadcasted_iota(jnp.int32, (SPAN, NY), 0) + LO
     above = jnp.where(gz > 0, LO, ZO)
@@ -241,15 +240,16 @@
             mask = jnp.logical_and(mask, inside)
         rden[plane, lo:hi, :] = jnp.where(mask, 1.0 / total, 0.0)
 
-    def sweep(source, target, skip=None, partial=None):
+    def sweep(source, target, end=None, level=None):
         def body(plane):
             mid = source[plane, LO:HI, :]
             side = cy[plane, LO:HI, :]
-            total = q[plane, LO:HI, :] if partial is None else part[partial, LO:HI, :]
-            if skip != -1:
-                total = total + cx[plane, LO:HI, :] * source[plane - 1, LO:HI, :]
-            if skip != 1:
+            if end is None:
+                total = q[plane, LO:HI, :] + cx[plane, LO:HI, :] * source[plane - 1, LO:HI, :]
                 total = total + cx[plane + 1, LO:HI, :] * source[plane + 1, LO:HI, :]
+            else:
+                total = part[4 + 2 * end + level, LO:HI, :]
+                total = total + cx[plane + 1 - end, LO:HI, :] * source[plane + 1 - 2 * end, LO:HI, :]
             total = total + cz[plane, LO:HI, :] * source[plane, LO - 1 : HI - 1, :]
             total = total + cz[plane, LO + 1 : HI + 1, :] * source[plane, LO + 1 : HI + 1, :]
             total = total + side * pltpu.roll(mid, NY - 1, 1) + pltpu.roll(side * mid, 1, 1)
@@ -266,7 +266,7 @@
     loaded(0)
     loaded(1)
     pl.semaphore_wait(barrier, beside)
-    send("zeps", "zpsi", "xpsi", "xeps", "dpsi", "deps")
+    send("zeps", "zpsi", "xpsi", "xeps")
 
     first, last = ZO + 8, ZO + NZL - 8
     blocked(lambda plane: face_x(plane, *MID), XO + 1, NXL - 1, 4)
@@ -292,9 +292,10 @@
         q[at] = 4.0 * (p_b[at] - n_b[at] + ions + q[at])
 
     blocked(charge, 0, NXL, 2)
-    send("zq", "xq", "dq", "zn", "zp", "zi")
+    send("zq", "xq", "zn", "zp", "zi")
 
     arrived("zeps")
+    send("ceps")
 
     def rim(body, low, high):
         def both(plane):
@@ -308,6 +309,7 @@
     blocked(rim(denominator, first, last), XO + 1, NXL - 2, 4)
     send("xrden")
     arrived("zpsi", "zq")
+    send("cpsi", "cq")
     both_sides(sweep(psi0, psi1), XO + 1, 2, 12)
     partial_sums(0, psi1)
     send("xpsi1", "xpart1")
@@ -325,41 +327,59 @@
     fields = (psi4, n_b, p_b, i_b)
     update = updater(fields, opt, height_ref, boundary, junction, depth)
 
+    def planes(body, first, count):
+        for u in range(count):
+            body(first + u)
+
+    def beside_face(end):
+        arrived("xeps", "ceps", side=end)
+        planes(lambda plane: face_x(plane, LO, HI), XO - 1 + 17 * end, 2)
+        planes(lambda plane: faces(plane, LO, HI), XO - 2 + 18 * end, 2)
+        inside = jnp.where(end == 0, gx, gxs - 1 - gx) > 0
+        for u in range(2):
+            plane = XO - 1 + 16 * end + u
+            own = jnp.logical_and(plane >= XO, plane < XO + NXL)
+            denominator(plane, LO, HI, jnp.logical_or(own, inside))
+        arrived("xpsi", "cpsi", "xq", "cq", side=end)
+        planes(sweep(psi0, psi1), XO - 1 + 16 * end, 2)
+
+    def close_to_face(end):
+        outer = XO - 2 + 19 * end
+        arrived("xrden", "xpsi1", "xpart1", side=end)
+        planes(sweep(psi1, psi2), XO - 1 + 15 * end, 3)
+        sweep(psi1, psi2, end, 0)(outer)
+        arrived("xpart2", side=end)
+        planes(sweep(psi2, psi3), XO - 1 + 14 * end, 4)
+        sweep(psi2, psi3, end, 1)(outer)
+        planes(sweep(psi3, psi4), XO - 1 + 13 * end, 5)
+
+    near, far = near_end(gx), 1 - near_end(gx)
+    beside_face(near)
+    close_to_face(near)
+    beside_face(far)
+    arrived("xn", "xp", "xi", side=near)
+
+    first = (NXL - DONE) * near
+
     def finish(k, flow):
         for u in range(2):
-            flow, result = update(EARLY + 2 * k + u, flow)
+            flow, result = update(first + 2 * k + u, flow)
             for ref, value in zip((n_s, p_s, i_s), result):
                 ref[2 * k + u] = value
         return flow
 
-    lax.fori_loop(0, DONE // 2, finish, face_flow(fields, EARLY))
-
-    arrived("xeps", "deps")
-    both_sides(lambda plane: face_x(plane, LO, HI), XO - 1, 2, 17)
-    both_sides(lambda plane: faces(plane, LO, HI), XO - 2, 2, 18)
-
-    def denominators(side, carry):
-        inside = jnp.where(side == 0, gx > 0, gx < gxs - 1)
-        for u in range(2):
-            plane = XO - 1 + side * 16 + u
-            own = jnp.logical_and(plane >= XO, plane < XO + NXL)
-            denominator(plane, LO, HI, jnp.logical_or(own, inside))
-        return carry
-
-    lax.fori_loop(0, 2, denominators, 0)
-    arrived("xpsi", "dpsi", "xq", "dq")
-    both_sides(sweep(psi0, psi1), XO - 1, 2, 16)
-    arrived("xrden", "xpsi1", "xpart1")
-    both_sides(sweep(psi1, psi2), XO - 1, 3, 15)
-    sweep(psi1, psi2, -1, 4)(XO - 2)
-    sweep(psi1, psi2, 1, 6)(XO + NXL + 1)
-    arrived("xpart2")
-    both_sides(sweep(psi2, psi3), XO - 1, 4, 14)
-    sweep(psi2, psi3, -1, 5)(XO - 2)
-    sweep(psi2, psi3, 1, 7)(XO + NXL + 1)
-    both_sides(sweep(psi3, psi4), XO - 1, 5, 13)
-    arrived("xn", "xp", "xi")
+    flow = lax.fori_loop(0, DONE // 2, finish, face_flow(fields, first))
+    if DONE % 2:
+        _, result = update(first + DONE - 1, flow)
+        for ref, value in zip((n_s, p_s, i_s), result):
+            ref[DONE - 1] = value
+    close_to_face(far)
+    arrived("xn", "xp", "xi", side=far)
     sent(*MESSAGES)
+
+
+def near_end(gx):
+    return 1 - lax.rem(gx, 2)
 
 
 def flux(a, b):
@@ -412,7 +432,7 @@
     psi_out, n_out, p_out, i_out,
     n_s, p_s, i_s, layer_ref, height_ref, map_sem, psi_sem, store_sem,
 ):
-    gz = lax.axis_index("gz")
+    gx, gz = lax.axis_index("gx"), lax.axis_index("gz")
     maps = (
         pltpu.make_async_copy(layer_h, layer_ref, map_sem.at[0]),
         pltpu.make_async_copy(height_h, height_ref, map_sem.at[1]),
@@ -422,9 +442,11 @@
     for x in range(NXL):
         pltpu.make_async_copy(psi.at[XO + x, pl.ds(ZO, NZL), :], psi_out.at[:, x, :], psi_sem).start()
     stores = ((n_s, n_d, n_out), (p_s, p_d, p_out), (i_s, i_d, i_out))
+    near = near_end(gx)
     for m, (_, done, target) in enumerate(stores):
         for k in range(DONE):
-            pltpu.make_async_copy(done.at[k], target.at[:, EARLY + k, :], store_sem.at[m]).start()
+            x = (NXL - DONE) * near + k
+            pltpu.make_async_copy(done.at[k], target.at[:, x, :], store_sem.at[m]).start()
 
     depth = (lax.broadcasted_iota(jnp.int32, (NZL, NY), 0) + gz * NZL).astype(F32)
     fields = (psi, n_b, p_b, i_b)
@@ -433,21 +455,18 @@
     boundary, junction = layer_counts(layer_ref)
     update = updater(fields, opt, height_ref, boundary, junction, depth)
 
-    def step(side, carry):
-        first = side * (EARLY + DONE)
-        flow = face_flow(fields, first)
-        for u in range(EARLY):
-            x = first + u
-            flow, result = update(x, flow)
-            for m, (source, _, target) in enumerate(stores):
-                source[x] = result[m]
-                pltpu.make_async_copy(source.at[x], target.at[:, x, :], store_sem.at[m]).start()
-        return carry
-
-    lax.fori_loop(0, 2, step, 0)
+    first = DONE * (1 - near)
+    flow = face_flow(fields, first)
+    for u in range(NXL - DONE):
+        x = first + u
+        flow, result = update(x, flow)
+        for m, (source, _, target) in enumerate(stores):
+            source[u] = result[m]
+            pltpu.make_async_copy(source.at[u], target.at[:, x, :], store_sem.at[m]).start()
     own = psi.at[pl.ds(XO, NXL), pl.ds(ZO, NZL), :]
     pltpu.make_async_copy(own, own, psi_sem).wait()
-    for k, (source, _, target) in enumerate(stores):
+    for k, (source, done, _) in enumerate(stores):
+        pltpu.make_async_copy(done, done, store_sem.at[k]).wait()
         pltpu.make_async_copy(source, source, store_sem.at[k]).wait()
 
 
@@ -482,7 +501,7 @@
         name="poisson",
     )(psi, eps, n, p, vac, dop, opt, layer, height)
     block = jax.ShapeDtypeStruct((NZL, NXL, NY), F32)
-    own = pltpu.VMEM((NXL, NZL, NY), F32)
+    own = pltpu.VMEM((NXL - DONE, NZL, NY), F32)
     return pl.pallas_call(
         transport_kernel,
         out_shape=[block] * 4,

time: 23.7 us -> 22 us (0.928)
  the two profiles are of different devices: /device:TPU:70 before, /device:TPU:100 now
where the time goes in v4:
time: 22 us; the launch traced here: 21.8 us
  Pallas kernels  21.2 us (96%)
  between operations  0.64 us (3%)
    pallas_call x1, Pallas kernels, on_device(): pl.pallas_call(poisson_kernel, out_shape=[planes] * 4 + [jax.ShapeDtypeSt...  17.7 us
    pallas_call x1, Pallas kernels, on_device(): pl.pallas_call(transport_kernel, out_shape=[block] * 4, in_specs=[near] *...  3.5 us

profile of v4, /device:TPU:100, one launch (start us, length us, event | category | flops | bytes accessed | tf_op | source)
XLA Modules:
  0.0 21.8 jit_solution(14834299488926002969)
XLA Ops:
  0.6 17.7 %poisson.1 = (f32[22,160,128]{2,1,0:T(8,128)S(1)}, f32[22,160,128]{2,1,0:T(8,128)S(1)}, f32[22,160,128]{2,1,0:T(8,128)S(1)}, f32[22,160,128]{2,1,0:T(8,128)S(1)}...) custom-call(f32[128,16,128]{2,1,0:T(8,128)} %psi_h.1, ...), custom_call_target="tpu_custom_call" | custom-call | tf_op jit(solution)/shard_map/poisson/pallas_call | solution.py:482
  18.3 3.5 %transport.1 = (f32[128,16,128]{2,1,0:T(8,128)}, f32[128,16,128]{2,1,0:T(8,128)}, f32[128,16,128]{2,1,0:T(8,128)}, f32[128,16,128]{2,1,0:T(8,128)}) custom-call(f32[22,160,128]{2,1,0:T(8,128)S(1)} %get-tuple-element.12.psi, f32[22,160,128]{2,1,0:T(8,128)S(1)} %get-tuple-element.13.n_b, f32[22,160,128]{2,1,0:T(8,128)S(1)} %get-tuple-element.14.p_b, ...), custom_call_target="tpu_custom_call" | custom-call | tf_op jit(solution)/shard_map/transport/pallas_call | solution.py:505

commit v5 on v4

--- a/solution.py
+++ b/solution.py
@@ -21,7 +21,7 @@
 HI = ZO + NZL + 8
 SPAN = HI - LO
 TINY = 1e-10
-DONE = 8
+DONE = 9
 
 XROWS = (ZO, ZO + NZL)
 
@@ -119,8 +119,8 @@
 
 def poisson_kernel(
     psi_h, eps_h, n_h, p_h, vac_h, dop_h, opt_h, layer_h, height_h,
-    psi4, n_b, p_b, i_b, opt, n_s, p_s, i_s,
-    psi0, psi1, psi2, psi3, eps, q, rden, cx, cy, cz, part, layer_ref, height_ref,
+    psi4, n_b, p_b, i_b, opt, layer_ref, height_ref, n_s, p_s, i_s,
+    psi0, psi1, psi2, psi3, eps, q, rden, cx, cy, cz, part,
     load_sem, map_sem, send_sem, recv_sem,
 ):
     gx, gz = lax.axis_index("gx"), lax.axis_index("gz")
@@ -157,8 +157,6 @@
     )
     for copy in maps:
         copy.start()
-    for x in range(NXL):
-        pltpu.make_async_copy(opt_h.at[:, x, :], opt.at[x], load_sem.at[6]).start()
 
     def loaded(k):
         target = inner(loads[k][1])
@@ -294,6 +292,8 @@
     blocked(charge, 0, NXL, 2)
     send("zq", "xq", "zn", "zp", "zi")
 
+    for x in range(NXL):
+        pltpu.make_async_copy(opt_h.at[:, x, :], opt.at[x], load_sem.at[6]).start()
     arrived("zeps")
     send("ceps")
 
@@ -363,16 +363,12 @@
 
     def finish(k, flow):
         for u in range(2):
-            flow, result = update(first + 2 * k + u, flow)
-            for ref, value in zip((n_s, p_s, i_s), result):
-                ref[2 * k + u] = value
+            flow = update(first + 2 * k + u, flow, (n_s, p_s, i_s), 2 * k + u)
         return flow
 
     flow = lax.fori_loop(0, DONE // 2, finish, face_flow(fields, first))
     if DONE % 2:
-        _, result = update(first + DONE - 1, flow)
-        for ref, value in zip((n_s, p_s, i_s), result):
-            ref[DONE - 1] = value
+        update(first + DONE - 1, flow, (n_s, p_s, i_s), DONE - 1)
     close_to_face(far)
     arrived("xn", "xp", "xi", side=far)
     sent(*MESSAGES)
@@ -402,43 +398,49 @@
 MID = (ZO, ZO + NZL)
 
 
+CHUNK = 64
+CHUNKS = tuple((ZO + r, ZO + r + CHUNK) for r in range(0, NZL, CHUNK))
+
+
 def face_flow(fields, x):
-    return flux(cells(fields, XO + x - 1, *MID), cells(fields, XO + x, *MID))
+    return tuple(flux(cells(fields, XO + x - 1, *c), cells(fields, XO + x, *c)) for c in CHUNKS)
 
 
 def updater(fields, opt, height_ref, boundary, junction, depth):
-    def update(x, before):
+    def update(x, before, targets, at):
         plane = XO + x
-        here = cells(fields, plane, *MID)
-        fx = flux(here, cells(fields, plane + 1, *MID))
-        fy = flux(here, tuple(pltpu.roll(f, NY - 1, 1) for f in here))
-        fz = flux(cells(fields, plane, ZO - 8, ZO + NZL), cells(fields, plane, ZO - 7, ZO + NZL + 1))
-        out = []
-        for k in range(3):
-            back = pltpu.roll(fz[k], 1, 0)[8:]
-            out.append(fx[k] - before[k] + fy[k] - pltpu.roll(fy[k], 1, 1) + fz[k][8:] - back)
-        _, n, p, i = here
         level = height_ref[pl.ds(x, 1), :].astype(F32)
-        rate = jnp.where(depth < boundary - level, 1.0, jnp.where(depth < junction - level, 10.0, 0.2))
-        loss = (n * p - 1.0) * rate / (n + p + 2.0)
-        gain = 0.05 * (opt[x] - loss)
-        return fx, (n - 0.04 * out[0] + gain, p - 0.03 * out[1] + gain, i - 0.02 * out[2])
+        flow = []
+        for (lo, hi), came in zip(CHUNKS, before):
+            rows = slice(lo - ZO, hi - ZO)
+            here = cells(fields, plane, lo, hi)
+            fx = flux(here, cells(fields, plane + 1, lo, hi))
+            fy = flux(here, tuple(pltpu.roll(f, NY - 1, 1) for f in here))
+            fz = flux(cells(fields, plane, lo - 8, hi), cells(fields, plane, lo - 7, hi + 1))
+            out = []
+            for k in range(3):
+                back = pltpu.roll(fz[k], 1, 0)[8:]
+                out.append(fx[k] - came[k] + fy[k] - pltpu.roll(fy[k], 1, 1) + fz[k][8:] - back)
+            _, n, p, i = here
+            z = depth[rows]
+            rate = jnp.where(z < boundary - level, 1.0, jnp.where(z < junction - level, 10.0, 0.2))
+            loss = (n * p - 1.0) * rate / (n + p + 2.0)
+            gain = 0.05 * (opt[x, rows, :] - loss)
+            targets[0][at, rows, :] = n - 0.04 * out[0] + gain
+            targets[1][at, rows, :] = p - 0.03 * out[1] + gain
+            targets[2][at, rows, :] = i - 0.02 * out[2]
+            flow.append(fx)
+        return tuple(flow)
 
     return update
 
 
 def transport_kernel(
-    psi, n_b, p_b, i_b, opt, n_d, p_d, i_d, layer_h, height_h,
+    psi, n_b, p_b, i_b, opt, layer_ref, height_ref, n_d, p_d, i_d,
     psi_out, n_out, p_out, i_out,
-    n_s, p_s, i_s, layer_ref, height_ref, map_sem, psi_sem, store_sem,
+    n_s, p_s, i_s, psi_sem, store_sem,
 ):
     gx, gz = lax.axis_index("gx"), lax.axis_index("gz")
-    maps = (
-        pltpu.make_async_copy(layer_h, layer_ref, map_sem.at[0]),
-        pltpu.make_async_copy(height_h, height_ref, map_sem.at[1]),
-    )
-    for copy in maps:
-        copy.start()
     for x in range(NXL):
         pltpu.make_async_copy(psi.at[XO + x, pl.ds(ZO, NZL), :], psi_out.at[:, x, :], psi_sem).start()
     stores = ((n_s, n_d, n_out), (p_s, p_d, p_out), (i_s, i_d, i_out))
@@ -450,8 +452,6 @@
 
     depth = (lax.broadcasted_iota(jnp.int32, (NZL, NY), 0) + gz * NZL).astype(F32)
     fields = (psi, n_b, p_b, i_b)
-    for copy in maps:
-        copy.wait()
     boundary, junction = layer_counts(layer_ref)
     update = updater(fields, opt, height_ref, boundary, junction, depth)
 
@@ -459,9 +459,8 @@
     flow = face_flow(fields, first)
     for u in range(NXL - DONE):
         x = first + u
-        flow, result = update(x, flow)
+        flow = update(x, flow, (n_s, p_s, i_s), u)
         for m, (source, _, target) in enumerate(stores):
-            source[u] = result[m]
             pltpu.make_async_copy(source.at[u], target.at[:, x, :], store_sem.at[m]).start()
     own = psi.at[pl.ds(XO, NXL), pl.ds(ZO, NZL), :]
     pltpu.make_async_copy(own, own, psi_sem).wait()
@@ -476,19 +475,18 @@
     psi, n, p, vac, eps, dop, opt, layer, height = far(psi, n, p, vac, eps, dop, opt, layer, height)
     anywhere = pl.BlockSpec(memory_space=pltpu.HBM)
     near = pl.BlockSpec(memory_space=pltpu.VMEM)
-    maps = [pltpu.VMEM((8, 128), jnp.int32), pltpu.VMEM((NXL, NY), jnp.int32)]
     planes = jax.ShapeDtypeStruct((PLANES, ROWS, NY), F32)
     field = pltpu.VMEM((PLANES, ROWS, NY), F32)
-    psi4, n_b, p_b, i_b, light, *done = pl.pallas_call(
+    psi4, n_b, p_b, i_b, light, *rest = pl.pallas_call(
         poisson_kernel,
         out_shape=[planes] * 4
         + [jax.ShapeDtypeStruct((NXL, NZL, NY), F32)]
+        + [jax.ShapeDtypeStruct((8, 128), jnp.int32), jax.ShapeDtypeStruct((NXL, NY), jnp.int32)]
         + [jax.ShapeDtypeStruct((DONE, NZL, NY), F32)] * 3,
         in_specs=[anywhere] * 9,
-        out_specs=[near] * 8,
+        out_specs=[near] * 10,
         scratch_shapes=[field] * 10
         + [pltpu.VMEM((8, ROWS, NY), F32)]
-        + maps
         + [
             pltpu.SemaphoreType.DMA((7,)),
             pltpu.SemaphoreType.DMA((2,)),
@@ -505,18 +503,16 @@
     return pl.pallas_call(
         transport_kernel,
         out_shape=[block] * 4,
-        in_specs=[near] * 8 + [anywhere] * 2,
+        in_specs=[near] * 10,
         out_specs=[anywhere] * 4,
         scratch_shapes=[own] * 3
         + [
-            *maps,
-            pltpu.SemaphoreType.DMA((2,)),
             pltpu.SemaphoreType.DMA,
             pltpu.SemaphoreType.DMA((3,)),
         ],
         compiler_params=pltpu.CompilerParams(vmem_limit_bytes=24 << 20),
         name="transport",
-    )(psi4, n_b, p_b, i_b, light, *done, layer, height)
+    )(psi4, n_b, p_b, i_b, light, *rest)
 
 
 def solution(mesh):

time: 22 us -> 21.4 us (0.973)
  the two profiles are of different devices: /device:TPU:100 before, /device:TPU:102 now
where the time goes in v5:
time: 21.4 us; the launch traced here: 21.2 us
  Pallas kernels  20.6 us (96%)
  between operations  0.64 us (3%)
    pallas_call x1, Pallas kernels, on_device(): pl.pallas_call(poisson_kernel, out_shape=[planes] * 4 + [jax.ShapeDtypeSt...  17.9 us
    pallas_call x1, Pallas kernels, on_device(): pl.pallas_call(transport_kernel, out_shape=[block] * 4, in_specs=[near] *...  2.65 us

profile of v5, /device:TPU:102, one launch (start us, length us, event | category | flops | bytes accessed | tf_op | source)
XLA Modules:
  0.0 21.2 jit_solution(13992269698558318791)
XLA Ops:
  0.6 17.9 %poisson.1 = (f32[22,160,128]{2,1,0:T(8,128)S(1)}, f32[22,160,128]{2,1,0:T(8,128)S(1)}, f32[22,160,128]{2,1,0:T(8,128)S(1)}, f32[22,160,128]{2,1,0:T(8,128)S(1)}...) custom-call(f32[128,16,128]{2,1,0:T(8,128)} %psi_h.1, ...), custom_call_target="tpu_custom_call" | custom-call | tf_op jit(solution)/shard_map/poisson/pallas_call | solution.py:480
  18.6 2.7 %transport.1 = (f32[128,16,128]{2,1,0:T(8,128)}, f32[128,16,128]{2,1,0:T(8,128)}, f32[128,16,128]{2,1,0:T(8,128)}, f32[128,16,128]{2,1,0:T(8,128)}) custom-call(f32[22,160,128]{2,1,0:T(8,128)S(1)} %get-tuple-element.14.psi, f32[22,160,128]{2,1,0:T(8,128)S(1)} %get-tuple-element.15.n_b, f32[22,160,128]{2,1,0:T(8,128)S(1)} %get-tuple-element.16.p_b, ...), custom_call_target="tpu_custom_call" | custom-call | tf_op jit(solution)/shard_map/transport/pallas_call | solution.py:503
